TPU v7x, 128 devices: a whole 4x4x4 slice. The times are simulated.
128 devices in a mesh: ctx: 32 (over z, x, core), head: 4 (over y).
Axes of the slice: x: 4, y: 4, z: 4, core: 2. Of those that a mesh axis runs over, the one named last changes fastest.
Arguments:
- queries: bfloat16 [384, 5120], P('ctx', 'head'), as said below
- draft_keys: bfloat16 [384, 1024], P('ctx', 'head'), may hold values from -2.5 to 2.5
- draft_values: bfloat16 [384, 1024], P('ctx', 'head'), may hold values from -6 to 6
- cache_keys: bfloat16 [2048, 128, 8, 128], P('ctx', None, 'head'), as said below
- cache_values: bfloat16 [2048, 128, 8, 128], P('ctx', None, 'head'), may hold values from -6 to 6
- w_out: bfloat16 [5120, 5120], P('head', 'ctx'), may hold values from -0.078125 to 0.078125
- lengths: int32 [24], replicated, may hold values from 1 to 65536, as said below
- block_req: int32 [2048], replicated, may hold values from 0 to 23, as said below
- block_idx: int32 [2048], replicated, may hold values from -1 to 511
- move_dst: int32 [2048], replicated, may hold values from -1 to 31, as said below
- draft_offs: int32 [24, 16], replicated, may hold values from 0 to 15, as said below
Outputs:
- mixed: bfloat16 [384, 5120], P('head', 'ctx')
- new_keys: bfloat16 [3072, 128, 8, 128], P('ctx', None, 'head')
- new_values: bfloat16 [3072, 128, 8, 128], P('ctx', None, 'head')
Inputs may be any that keep to these rules, and one draw needn't show every extreme that they name: queries lie within -6 to 6. cache_keys lie within -6 to 6. Request r has exactly ceil(lengths[r] / 128) blocks, numbered from 0, each in exactly one slot. Empty slots hold block_req 0; on each index of ctx the live slots come before the empty ones. `move_dst`: only live blocks move, never to their own index; at most 2 blocks go from one index of ctx to one other and at most 32 arrive at one index, both reached. draft_offs[r, t] <= t.
All inputs are finite; a program needn't handle non-finite values.
Results may differ from a plain program's by a relative error of at most 0.0051.
Values may be sent and summed in bfloat16 or wider, within the bound.
No kernel may reach another device: no remote copies, remote signals or barrier semaphores. Data moves between devices by JAX's collectives and lax.ppermute only.
A program may use at most 128 MiB of HBM per device.

v0:
```python
import functools
import math

import jax
import jax.numpy as jnp
from jax import lax
from jax.experimental import pallas as pl
from jax.experimental.pallas import tpu as pltpu
from jax.sharding import PartitionSpec as P

CAP = 2
STEP = 4
LOW = -1e30


def pack_kernel(rank_ref, dst_ref, k_ref, v_ref, send_ref, used, sems):
    blocks = k_ref.shape[0]
    base = rank_ref[0] * blocks

    def clear(d, carry):
        used[d] = 0
        return carry

    lax.fori_loop(0, used.shape[0], clear, 0)

    def copies(b, dst, place):
        return (
            pltpu.make_async_copy(k_ref.at[b], send_ref.at[dst, place, 0], sems.at[b, 0]),
            pltpu.make_async_copy(v_ref.at[b], send_ref.at[dst, place, 1], sems.at[b, 1]),
        )

    def start(b, carry):
        dst = dst_ref[base + b]

        @pl.when(dst >= 0)
        def _():
            place = jnp.minimum(used[dst], CAP - 1)
            used[dst] = place + 1
            for c in copies(b, dst, place):
                c.start()

        return carry

    lax.fori_loop(0, blocks, start, 0)

    def finish(b, carry):
        @pl.when(dst_ref[base + b] >= 0)
        def _():
            for c in copies(b, 0, 0):
                c.wait()

        return carry

    lax.fori_loop(0, blocks, finish, 0)


def pack(rank, move_dst, keys, values, nctx):
    blocks, rows, lanes = keys.shape
    return pl.pallas_call(
        pack_kernel,
        out_shape=jax.ShapeDtypeStruct((nctx, CAP, 2, rows, lanes), keys.dtype),
        grid_spec=pltpu.PrefetchScalarGridSpec(
            num_scalar_prefetch=2,
            grid=(1,),
            in_specs=[pl.BlockSpec((blocks, rows, lanes), lambda i, *_: (0, 0, 0))] * 2,
            out_specs=pl.BlockSpec(memory_space=pltpu.HBM),
            scratch_shapes=[
                pltpu.SMEM((nctx,), jnp.int32),
                pltpu.SemaphoreType.DMA((blocks, 2)),
            ],
        ),
        compiler_params=pltpu.CompilerParams(vmem_limit_bytes=40 * 2**20),
        cost_estimate=pl.CostEstimate(
            flops=0, bytes_accessed=4 * blocks * rows * lanes * 2, transcendentals=0
        ),
        name="pack",
    )(rank, move_dst, keys, values)


def unpack_kernel(slots, count_ref, recv_ref, _k, _v, k_out, v_out, stage, loads, stores):
    nctx = count_ref.shape[0]
    first = k_out.shape[0] - slots
    outs = (k_out, v_out)

    def load(row, place, slot, i):
        return pltpu.make_async_copy(
            recv_ref.at[row, place, i], stage.at[slot, i], loads.at[slot, i]
        )

    def store(slot, i):
        return pltpu.make_async_copy(stage.at[slot, i], outs[i].at[first + slot], stores.at[slot, i])

    def source(s, slot):
        count = count_ref[s]
        for place in range(CAP):

            @pl.when((count > place) & (slot + place < slots))
            def _():
                for i in range(2):
                    load(s, place, slot + place, i).start()

        return slot + count

    filled = jnp.minimum(lax.fori_loop(0, nctx, source, 0), slots)

    def blank(slot, carry):
        stage[slot] = jnp.zeros(stage.shape[1:], stage.dtype)
        for i in range(2):
            store(slot, i).start()
        return carry

    lax.fori_loop(filled, slots, blank, 0)

    def passed(slot, carry):
        for i in range(2):
            load(0, 0, slot, i).wait()
            store(slot, i).start()
        return carry

    lax.fori_loop(0, filled, passed, 0)

    def finish(slot, carry):
        for i in range(2):
            store(slot, i).wait()
        return carry

    lax.fori_loop(0, slots, finish, 0)


def unpack(count, recv, keys, values, slots):
    rows, lanes = keys.shape[1:]
    shape = jax.ShapeDtypeStruct(keys.shape, keys.dtype)
    return pl.pallas_call(
        functools.partial(unpack_kernel, slots),
        out_shape=(shape, shape),
        grid_spec=pltpu.PrefetchScalarGridSpec(
            num_scalar_prefetch=1,
            grid=(1,),
            in_specs=[pl.BlockSpec(memory_space=pltpu.HBM)] * 3,
            out_specs=[pl.BlockSpec(memory_space=pltpu.HBM)] * 2,
            scratch_shapes=[
                pltpu.VMEM((slots, 2, rows, lanes), keys.dtype),
                pltpu.SemaphoreType.DMA((slots, 2)),
                pltpu.SemaphoreType.DMA((slots, 2)),
            ],
        ),
        input_output_aliases={2: 0, 3: 1},
        cost_estimate=pl.CostEstimate(
            flops=0, bytes_accessed=8 * slots * rows * lanes, transcendentals=0
        ),
        name="unpack",
    )(count, recv, keys, values)


def attend(q, keys, values, column, limit, top, total, numer, r, log_scale):
    scores = lax.dot_general(q, keys, (((1,), (1,)), ((), ())), preferred_element_type=jnp.float32)
    scores = jnp.where(column < limit, scores, LOW)
    best = jnp.max(scores, axis=1, keepdims=True)
    best = best.astype(jnp.bfloat16).astype(jnp.float32)
    old = top[r]
    new = jnp.maximum(old, best)
    probs = jnp.exp2((scores - new[:, :1]) * log_scale)
    shrink = jnp.exp2((old - new) * log_scale)
    top[r] = new
    lanes = numer.shape[2]
    width = probs.shape[1]
    if width > lanes:
        part = probs[:, :lanes]
        for first in range(lanes, width, lanes):
            part = part + probs[:, first : first + lanes]
    else:
        part = jnp.concatenate(
            [probs, jnp.zeros((probs.shape[0], lanes - width), jnp.float32)], axis=1
        )
    total[r] = total[r] * shrink + part
    numer[r] = numer[r] * shrink + jnp.dot(
        probs.astype(jnp.bfloat16), values, preferred_element_type=jnp.float32
    )


def attention_kernel(
    kv_local, group, log_scale,
    rank_ref, req_ref, idx_ref, dst_ref, len_ref,
    q_ref, dk_ref, dv_ref, offs_ref, k_ref, v_ref,
    numer_ref, stats_ref, k_out, v_out,
    top, total, numer, column,
):
    step = pl.program_id(0)
    requests, rows, lanes = numer.shape
    width = k_ref.shape[1] // kv_local
    blocks = pl.num_programs(0) * STEP
    rank = rank_ref[0]
    base = rank * blocks + step * STEP

    @pl.when(step == 0)
    def _():
        top[...] = jnp.full(top.shape, LOW, jnp.float32)
        total[...] = jnp.zeros(total.shape, jnp.float32)
        numer[...] = jnp.zeros(numer.shape, jnp.float32)
        line = lax.broadcasted_iota(jnp.int32, column.shape, 1)
        row = lax.broadcasted_iota(jnp.int32, column.shape, 0)
        own = row % (kv_local * group) // group
        column[...] = jnp.where(line % kv_local == own, line // kv_local, 1 << 20)

        @pl.when(rank < requests)
        def _():
            drafts = dk_ref.shape[1]
            spot = column[:, :drafts]
            spot = jnp.where(spot >= offs_ref[...], spot, 1 << 20)
            token = lax.broadcasted_iota(jnp.int32, spot.shape, 0) // (kv_local * group)
            attend(q_ref[rank], dk_ref[rank], dv_ref[rank], spot, token + 1,
                   top, total, numer, rank, log_scale)

    for g in range(STEP):
        slot = base + g
        stays = dst_ref[slot] < 0

        @pl.when(stays)
        def _():
            k_out[g] = k_ref[g]
            v_out[g] = v_ref[g]

        @pl.when(jnp.logical_not(stays))
        def _():
            k_out[g] = jnp.zeros(k_out.shape[1:], k_out.dtype)
            v_out[g] = jnp.zeros(v_out.shape[1:], v_out.dtype)

        idx = idx_ref[slot]

        @pl.when(idx >= 0)
        def _():
            r = req_ref[slot]
            limit = jnp.minimum(len_ref[r] - idx * width, width)
            attend(q_ref[r], k_ref[g], v_ref[g], column[...], limit,
                   top, total, numer, r, log_scale)

    @pl.when(step == pl.num_programs(0) - 1)
    def _():
        ones = jnp.ones((8, lanes), jnp.float32)
        first = (lax.broadcasted_iota(jnp.int32, (8, lanes), 1) == 0).astype(jnp.float32)
        pick = lax.broadcasted_iota(jnp.int32, (8, rows), 0)
        turn = (((1,), (1,)), ((), ()))

        def close(r, carry):
            numer_ref[r] = numer[r].astype(numer_ref.dtype)
            sums = lax.dot_general(ones, total[r], turn, precision=lax.Precision.HIGHEST,
                                   preferred_element_type=jnp.float32)
            tops = lax.dot_general(first, top[r], turn, precision=lax.Precision.HIGHEST,
                                   preferred_element_type=jnp.float32)
            stats_ref[r] = jnp.where(pick == 0, tops, sums)
            return carry

        lax.fori_loop(0, requests, close, 0)


def attention(rank, block_req, block_idx, move_dst, lengths, q, dk, dv, offs, keys, values,
              slots, kv_local, group, log_scale):
    blocks, width, lanes = keys.shape
    requests, rows, _ = q.shape
    whole = lambda shape: pl.BlockSpec(shape, lambda i, *_: (0,) * len(shape))
    part = pl.BlockSpec((STEP, width, lanes), lambda i, *_: (i, 0, 0))
    cache = jax.ShapeDtypeStruct((blocks + slots, width, lanes), keys.dtype)
    return pl.pallas_call(
        functools.partial(attention_kernel, kv_local, group, log_scale),
        out_shape=(
            jax.ShapeDtypeStruct((requests, rows, lanes), jnp.float32),
            jax.ShapeDtypeStruct((requests, 8, rows), jnp.float32),
            cache,
            cache,
        ),
        grid_spec=pltpu.PrefetchScalarGridSpec(
            num_scalar_prefetch=5,
            grid=(blocks // STEP,),
            in_specs=[whole(q.shape), whole(dk.shape), whole(dv.shape), whole(offs.shape), part, part],
            out_specs=[whole((requests, rows, lanes)), whole((requests, 8, rows)), part, part],
            scratch_shapes=[
                pltpu.VMEM((requests, rows, lanes), jnp.float32),
                pltpu.VMEM((requests, rows, lanes), jnp.float32),
                pltpu.VMEM((requests, rows, lanes), jnp.float32),
                pltpu.VMEM((rows, width), jnp.int32),
            ],
        ),
        compiler_params=pltpu.CompilerParams(vmem_limit_bytes=40 * 2**20),
        cost_estimate=pl.CostEstimate(
            flops=4 * blocks * rows * width * lanes,
            bytes_accessed=8 * blocks * width * lanes,
            transcendentals=blocks * rows * width,
        ),
        name="attention",
    )(rank, block_req, block_idx, move_dst, lengths, q, dk, dv, offs, keys, values)


def exchange(x, axis, groups=None):
    return lax.all_to_all(
        x, axis, split_axis=0, concat_axis=0, tiled=True, axis_index_groups=groups
    )


def everywhere(x, axis, groups):
    return exchange(jnp.broadcast_to(x[None], (len(groups[0]), *x.shape)), axis, groups)


def across(x, axis):
    return lax.ppermute(x, axis, [(i, i ^ 1) for i in range(lax.axis_size(axis))])


def shards(
    queries, draft_keys, draft_values, cache_keys, cache_values, w_out,
    lengths, block_req, block_idx, move_dst, draft_offs,
):
    blocks, width, kv_local, head_dim = cache_keys.shape
    nctx = lax.axis_size("ctx")
    rank = lax.axis_index("ctx").astype(jnp.int32)
    requests, drafts = draft_offs.shape
    own = queries.shape[0]
    heads = queries.shape[1] // head_dim
    group = heads // kv_local
    tokens = requests * drafts
    slots = nctx
    log_scale = math.log2(math.e) / math.sqrt(head_dim)
    me = rank.reshape(1)

    keys = cache_keys.reshape(blocks, width * kv_local, head_dim)
    values = cache_values.reshape(blocks, width * kv_local, head_dim)

    mine = jnp.concatenate(
        [
            queries.reshape(own * heads, head_dim),
            draft_keys.reshape(own * kv_local, head_dim),
            draft_values.reshape(own * kv_local, head_dim),
        ],
        axis=0,
    )
    chips = nctx // 2
    odd = rank % 2 == 1
    sides = [[2 * i + side for i in range(chips)] for side in range(2)]
    send = pack(me, move_dst, keys, values, nctx)
    same = everywhere(mine, "ctx", sides)
    same, send = lax.optimization_barrier((same, send))
    recv = exchange(send, "ctx")
    other = across(same, "ctx")
    shared = jnp.where(odd, jnp.stack([other, same], axis=1), jnp.stack([same, other], axis=1))
    shared = shared.reshape(nctx, -1, head_dim)
    cut = own * heads
    cut2 = cut + own * kv_local
    q = shared[:, :cut].reshape(requests, drafts * heads, head_dim)
    dk = shared[:, cut:cut2].reshape(requests, drafts * kv_local, head_dim)
    dv = shared[:, cut2:].reshape(requests, drafts * kv_local, head_dim)

    my_offs = lax.dynamic_slice_in_dim(draft_offs, jnp.minimum(rank, requests - 1), 1)[0]
    offs = jnp.repeat(my_offs, heads)[:, None]
    numer, stats, new_keys, new_values = attention(
        me, block_req, block_idx, move_dst, lengths, q, dk, dv, offs, keys, values,
        slots, kv_local, group, log_scale,
    )
    rows = own * heads

    def halves(x):
        x = x.reshape(chips, 2, *x.shape[1:])
        return jnp.where(odd, x[:, 1], x[:, 0]), jnp.where(odd, x[:, 0], x[:, 1])

    kept, given = halves(numer.reshape(nctx, rows, head_dim))
    kept_notes, given_notes = halves(
        jnp.swapaxes(stats[:, :2], 0, 1).reshape(2, nctx, rows).swapaxes(0, 1)
    )
    taken, taken_notes = across(given, "ctx"), across(given_notes, "ctx")
    pair_top = jnp.maximum(kept_notes[:, 0], taken_notes[:, 0])
    fa = jnp.exp2((kept_notes[:, 0] - pair_top) * log_scale)
    fb = jnp.exp2((taken_notes[:, 0] - pair_top) * log_scale)
    pair = (kept * fa[:, :, None] + taken * fb[:, :, None]).astype(jnp.bfloat16)
    sums = kept_notes[:, 1] * fa + taken_notes[:, 1] * fb
    high = sums.astype(jnp.bfloat16)
    rest = (sums - high.astype(jnp.float32)).astype(jnp.bfloat16)
    notes = jnp.stack([pair_top.astype(jnp.bfloat16), high, rest], axis=1)
    notes = jnp.pad(notes, ((0, 0), (0, 5), (0, head_dim - rows)))
    packet = jnp.concatenate([pair, notes], axis=1)
    packet, recv = lax.optimization_barrier((packet, recv))
    parts = exchange(packet, "ctx", sides)
    count = jnp.sum((move_dst.reshape(nctx, blocks) == rank).astype(jnp.int32), axis=1)
    new_keys, new_values = unpack(count, recv, new_keys, new_values, slots)
    notes = parts[:, rows : rows + 3, :rows].astype(jnp.float32)
    top = jnp.max(notes[:, 0], axis=0)
    factor = jnp.exp2((notes[:, 0] - top) * log_scale)
    denom = jnp.sum(factor * (notes[:, 1] + notes[:, 2]), axis=0)
    total = jnp.sum(parts[:, :rows].astype(jnp.float32) * factor[:, :, None], axis=0)
    attn = (total / denom[:, None]).astype(jnp.bfloat16)
    same = everywhere(attn.reshape(own, heads * head_dim), "ctx", sides)
    other = across(same, "ctx")

    def project(x):
        x = x.reshape(chips * own, heads * head_dim)
        y = jnp.dot(x, w_out, preferred_element_type=jnp.float32)
        return y.reshape(chips, own, -1)

    same, other = project(same), project(other)
    partial = jnp.where(odd, jnp.stack([other, same], axis=1), jnp.stack([same, other], axis=1))
    nhead = lax.axis_size("head")
    shares = exchange(partial.reshape(nhead, tokens // nhead, -1), "head")
    mixed = functools.reduce(jnp.add, [shares[i] for i in range(nhead)]).astype(jnp.bfloat16)
    shape = (blocks + slots, width, kv_local, head_dim)
    return (mixed, new_keys.reshape(shape), new_values.reshape(shape))


def solution(mesh):
    cache = P("ctx", None, "head", None)
    in_specs = (
        P("ctx", "head"), P("ctx", "head"), P("ctx", "head"), cache, cache, P("head", "ctx"),
        P(), P(), P(), P(), P(),
    )
    out_specs = (P("head", "ctx"), cache, cache)
    return jax.shard_map(shards, mesh=mesh, in_specs=in_specs, out_specs=out_specs, check_vma=False)
```

profile of v0, /device:TPU:1, one launch (start us, length us, event | category | flops | bytes accessed | tf_op | source)
XLA Modules:
  0.0 181.2 jit_solution(4718359587693851391)
XLA Ops:
  0.7 0.8 reshape.150
  1.4 0.7 reshape.149
  2.1 0.8 reshape.148
  3.0 0.9 broadcast_in_dim.6
  3.9 8.4 %all-to-all-start = ((bf16[16,168,128]{2,1,0:T(8,128)(2,1)}), bf16[16,168,128]{2,1,0:T(8,128)(2,1)S(1)}, u32[]{:S(2)}, u32[]{:S(2)}) async-start(bf16[16,168,128]{2,1,0:T(8,128)(2,1)} %broadcast_in_dim.6), calls=%async_computation | async-start | bytes 1376256 | tf_op jit(solution)/shard_map/all_to_all | solution.py:294
  12.4 2.2 %copy-done.1 = bf16[64,128,2,128]{3,2,1,0:T(2,128)(2,1)S(1)} copy-done((bf16[64,128,2,128]{3,2,1,0:T(2,128)(2,1)S(1)}, bf16[64,128,2,128]{3,2,1,0:T(2,128)(2,1)}, u32[]{:S(2)}) %copy-start.1) | copy-done | bytes 4194328
  14.6 2.2 %copy-done.3 = bf16[64,128,2,128]{3,2,1,0:T(2,128)(2,1)S(1)} copy-done((bf16[64,128,2,128]{3,2,1,0:T(2,128)(2,1)S(1)}, bf16[64,128,2,128]{3,2,1,0:T(2,128)(2,1)}, u32[]{:S(2)}) %copy-start.3) | copy-done | bytes 4194328
  16.8 4.3 %pack.1 = bf16[32,2,2,256,128]{4,3,2,1,0:T(8,128)(2,1)} custom-call(s32[1]{0:T(128)} %bitcast.rank_ref, s32[2048]{0:T(1024)S(1)} %copy-done.5, bf16[64,256,128]{2,1,0:T(8,128)(2,1)S(1)} %bitcast.80, bf16[64,256,128]{2,1,0:T(8,128)(2,1)S(1)} %bitcast.82), custom_call_target="tpu_custom_call" | custom-call | bytes 16777216 | tf_op jit(solution)/shard_map/pack/pallas_call | solution.py:59
  21.1 3.4 %all-to-all-done = bf16[16,168,128]{2,1,0:T(8,128)(2,1)S(1)} async-done(((bf16[16,168,128]{2,1,0:T(8,128)(2,1)}), bf16[16,168,128]{2,1,0:T(8,128)(2,1)S(1)}, u32[]{:S(2)}, u32[]{:S(2)}) %all-to-all-start) | async-done | bytes 688160 | tf_op jit(solution)/shard_map/all_to_all | solution.py:294
  24.5 6.7 %all-to-all-start.1 = ((bf16[32,2,2,256,128]{4,3,2,1,0:T(8,128)(2,1)}), bf16[32,2,2,256,128]{4,3,2,1,0:T(8,128)(2,1)}, u32[]{:S(2)}, u32[]{:S(2)}) async-start(bf16[32,2,2,256,128]{4,3,2,1,0:T(8,128)(2,1)} %pack.1), calls=%async_computation.1 | async-start | bytes 16777216 | tf_op jit(solution)/shard_map/all_to_all | solution.py:294
  31.2 0.5 collective-permute-start
  31.7 0.2 dynamic-slice_reduce_fusion
  31.8 0.1 broadcast_in_dim.7
  31.9 0.1 broadcast_in_dim_reshape.5.offs_ref
  32.0 1.4 collective-permute-done
  33.4 0.3 maximum_select_fusion
  33.8 0.1 slice.91
  33.9 1.7 copy-done.2
  35.6 2.2 %copy-done.4 = bf16[64,128,2,128]{3,2,1,0:T(2,128)(2,1)S(1)} copy-done((bf16[64,128,2,128]{3,2,1,0:T(2,128)(2,1)S(1)}, bf16[64,128,2,128]{3,2,1,0:T(2,128)(2,1)}, u32[]{:S(2)}) %copy-start.4) | copy-done | bytes 4194328
  37.8 43.4 %attention.1 = (f32[24,160,128]{2,1,0:T(8,128)S(1)}, f32[24,8,160]{2,1,0:T(8,128)S(1)}, bf16[96,256,128]{2,1,0:T(8,128)(2,1)}, bf16[96,256,128]{2,1,0:T(8,128)(2,1)}) custom-call(s32[1]{0:T(128)} %bitcast.rank_ref, s32[2048]{0:T(1024)S(1)} %copy-done.6, s32[2048]{0:T(1024)S(1)} %copy-done.7, s32[2048]{0:T(1024)S(1)} %copy-done.5, s32[24]{0:T(128)S(1)} %copy-done.8, ...), custom_call_target="tpu_custom_call" | custom-call | flops 1342177280 | bytes 16777216 | tf_op jit(solution)/shard_map/attention/pallas_call | solution.py:263
  81.3 0.1 reshape.156
  81.4 0.1 collective-permute-start.1
  81.5 0.1 select_bitcast_fusion
  81.6 0.6 collective-permute-start.2
  82.2 0.5 collective-permute-done.1
  82.7 1.6 collective-permute-done.2
  84.4 0.7 fusion.2
  85.0 0.1 fusion.3
  85.1 45.9 %all-to-all-done.1.recv_ref = bf16[32,2,2,256,128]{4,3,2,1,0:T(8,128)(2,1)} async-done(((bf16[32,2,2,256,128]{4,3,2,1,0:T(8,128)(2,1)}), bf16[32,2,2,256,128]{4,3,2,1,0:T(8,128)(2,1)}, u32[]{:S(2)}, u32[]{:S(2)}) %all-to-all-start.1) | async-done | bytes 8388640 | tf_op jit(solution)/shard_map/all_to_all | solution.py:294
  130.9 18.0 %all_to_all.25 = bf16[16,128,128]{2,1,0:T(8,128)(2,1)S(1)} all-to-all(bf16[16,128,128]{2,1,0:T(8,128)(2,1)S(1)} %fusion.3), channel_id=1, replica_groups={{0,8,16,24,32,40,48,56,64,72,80,88,96,104,112,120},{4,12,20,28,36,44,52..., dimensions={0} | all-to-all | bytes 1048576 | tf_op jit(solution)/shard_map/all_to_all | solution.py:294
  149.0 0.3 multiply_reduce_fusion
  149.4 0.1 div.16
  149.4 0.1 div.17
  149.7 13.8 %all_to_all.26 = bf16[16,12,1280]{2,1,0:T(8,128)(2,1)S(1)} all-to-all(bf16[16,12,1280]{2,1,0:T(8,128)(2,1)S(1)} %broadcast_in_dim.8), channel_id=1, replica_groups={{0,8,16,24,32,40,48,56,64,72,80,88,96,104,112,120},{4,12,20,28,36,44,52..., dimensions={0} | all-to-all | bytes 983040 | tf_op jit(solution)/shard_map/all_to_all | solution.py:294
  163.5 0.1 copy.59
  163.6 3.2 %collective-permute-start.3 = (bf16[16,12,1280]{2,0,1:T(8,128)(2,1)S(1)}, bf16[16,12,1280]{2,0,1:T(8,128)(2,1)S(1)}, u32[]{:S(2)}, u32[]{:S(2)}) collective-permute-start(bf16[16,12,1280]{2,0,1:T(8,128)(2,1)S(1)} %copy.59), channel_id=1, source_target_pairs={{0,4},{4,0},{8,12},{12,8},{16,20},{20,16},{24,28},{28,24},{32,36},... | collective-permute-start | bytes 1474568 | tf_op jit(solution)/shard_map/ppermute | solution.py:304
  166.8 0.3 fusion.4
  167.2 0.1 copy.71
  167.3 1.0 collective-permute-done.3
  168.3 0.3 convolution_bitcast_fusion
  168.6 0.2 copy.61
  168.9 0.9 copy.62
  169.9 4.2 %all-to-all-start.4 = ((f32[4,96,160]{1,2,0:T(8,128)}), f32[4,96,160]{1,2,0:T(8,128)S(1)}, u32[]{:S(2)}, u32[]{:S(2)}) async-start(f32[4,96,160]{1,2,0:T(8,128)} %copy.62), calls=%async_computation.4 | async-start | bytes 655360 | tf_op jit(solution)/shard_map/all_to_all | solution.py:294
  174.1 0.1 reshape.160
  174.1 0.6 reduce_sum.32.count_ref
  174.8 4.3 %unpack.1 = (bf16[96,256,128]{2,1,0:T(8,128)(2,1)}, bf16[96,256,128]{2,1,0:T(8,128)(2,1)}) custom-call(s32[32]{0:T(128)} %reduce_sum.32.count_ref, bf16[32,2,2,256,128]{4,3,2,1,0:T(8,128)(2,1)} %all-to-all-done.1.recv_ref, bf16[96,256,128]{2,1,0:T(8,128)(2,1)} %get-tuple-element.19._k, ...), custom_call_target="tpu_custom_call", output_to_operand_aliasing={{0}: (2, {}), {1}: (3, {})} | custom-call | bytes 8388608 | tf_op jit(solution)/shard_map/unpack/pallas_call | solution.py:133
  179.0 1.5 all-to-all-done.4
  180.6 0.6 fusion.8
  (39 shorter events, 0.5 us)
Async XLA Ops:
  0.6 166.2 %copy-start = (bf16[1280,160]{0,1:T(8,128)(2,1)S(1)}, bf16[1280,160]{0,1:T(8,128)(2,1)}, u32[]{:S(2)}) copy-start(bf16[1280,160]{0,1:T(8,128)(2,1)} %param.16) | copy-start | bytes 1228804
  0.6 11.7 %copy-start.5 = (s32[2048]{0:T(1024)S(1)}, s32[2048]{0:T(1024)}, u32[]{:S(2)}) copy-start(s32[2048]{0:T(1024)} %dst_ref.3) | copy-start | bytes 24580
  3.9 20.6 %all-to-all-start = ((bf16[16,168,128]{2,1,0:T(8,128)(2,1)}), bf16[16,168,128]{2,1,0:T(8,128)(2,1)S(1)}, u32[]{:S(2)}, u32[]{:S(2)}) async-start(bf16[16,168,128]{2,1,0:T(8,128)(2,1)} %broadcast_in_dim.6), calls=%async_computation | async-start | bytes 1376256 | tf_op jit(solution)/shard_map/all_to_all | solution.py:294
  12.4 2.2 %copy-start.1 = (bf16[64,128,2,128]{3,2,1,0:T(2,128)(2,1)S(1)}, bf16[64,128,2,128]{3,2,1,0:T(2,128)(2,1)}, u32[]{:S(2)}) copy-start(bf16[64,128,2,128]{3,2,1,0:T(2,128)(2,1)} %param.14) | copy-start | bytes 12582916
  14.6 2.2 %copy-start.3 = (bf16[64,128,2,128]{3,2,1,0:T(2,128)(2,1)S(1)}, bf16[64,128,2,128]{3,2,1,0:T(2,128)(2,1)}, u32[]{:S(2)}) copy-start(bf16[64,128,2,128]{3,2,1,0:T(2,128)(2,1)} %param.15) | copy-start | bytes 12582916
  21.1 10.6 %copy-start.9 = (s32[24,16]{0,1:T(8,128)S(1)}, s32[24,16]{0,1:T(8,128)}, u32[]{:S(2)}) copy-start(s32[24,16]{0,1:T(8,128)} %param.21) | copy-start | bytes 4612
  24.5 106.5 %all-to-all-start.1 = ((bf16[32,2,2,256,128]{4,3,2,1,0:T(8,128)(2,1)}), bf16[32,2,2,256,128]{4,3,2,1,0:T(8,128)(2,1)}, u32[]{:S(2)}, u32[]{:S(2)}) async-start(bf16[32,2,2,256,128]{4,3,2,1,0:T(8,128)(2,1)} %pack.1), calls=%async_computation.1 | async-start | bytes 16777216 | tf_op jit(solution)/shard_map/all_to_all | solution.py:294
  31.2 2.3 %collective-permute-start = (bf16[16,168,128]{2,1,0:T(8,128)(2,1)S(1)}, bf16[16,168,128]{2,1,0:T(8,128)(2,1)S(1)}, u32[]{:S(2)}, u32[]{:S(2)}) collective-permute-start(bf16[16,168,128]{2,1,0:T(8,128)(2,1)S(1)} %all-to-all-done), channel_id=1, source_target_pairs={{0,4},{4,0},{8,12},{12,8},{16,20},{20,16},{24,28},{28,24},{32,36},... | collective-permute-start | bytes 2064392 | tf_op jit(solution)/shard_map/ppermute | solution.py:304
  33.4 2.2 %copy-start.2 = (bf16[64,128,2,128]{3,2,1,0:T(2,128)(2,1)S(1)}, bf16[64,128,2,128]{3,2,1,0:T(2,128)(2,1)}, u32[]{:S(2)}) copy-start(bf16[64,128,2,128]{3,2,1,0:T(2,128)(2,1)} %param.14) | copy-start | bytes 12582916
  33.7 1.9 %copy-start.6 = (s32[2048]{0:T(1024)S(1)}, s32[2048]{0:T(1024)}, u32[]{:S(2)}) copy-start(s32[2048]{0:T(1024)} %req_ref.1) | copy-start | bytes 24580
  33.7 1.9 %copy-start.7 = (s32[2048]{0:T(1024)S(1)}, s32[2048]{0:T(1024)}, u32[]{:S(2)}) copy-start(s32[2048]{0:T(1024)} %idx_ref.1) | copy-start | bytes 24580
  33.7 1.9 %copy-start.8 = (s32[24]{0:T(128)S(1)}, s32[24]{0:T(128)}, u32[]{:S(2)}) copy-start(s32[24]{0:T(128)} %len_ref.1) | copy-start | bytes 292
  35.6 2.2 %copy-start.4 = (bf16[64,128,2,128]{3,2,1,0:T(2,128)(2,1)S(1)}, bf16[64,128,2,128]{3,2,1,0:T(2,128)(2,1)}, u32[]{:S(2)}) copy-start(bf16[64,128,2,128]{3,2,1,0:T(2,128)(2,1)} %param.15) | copy-start | bytes 12582916
  81.4 1.3 collective-permute-start.1
  81.6 2.8 %collective-permute-start.2 = (f32[16,120,128]{2,1,0:T(8,128)S(1)}, f32[16,120,128]{2,1,0:T(8,128)S(1)}, u32[]{:S(2)}, u32[]{:S(2)}) collective-permute-start(f32[16,120,128]{2,1,0:T(8,128)S(1)} %select_bitcast_fusion), channel_id=1, source_target_pairs={{0,4},{4,0},{8,12},{12,8},{16,20},{20,16},{24,28},{28,24},{32,36},... | collective-permute-start | bytes 2949128 | tf_op jit(solution)/shard_map/ppermute | solution.py:304
  163.6 4.7 %collective-permute-start.3 = (bf16[16,12,1280]{2,0,1:T(8,128)(2,1)S(1)}, bf16[16,12,1280]{2,0,1:T(8,128)(2,1)S(1)}, u32[]{:S(2)}, u32[]{:S(2)}) collective-permute-start(bf16[16,12,1280]{2,0,1:T(8,128)(2,1)S(1)} %copy.59), channel_id=1, source_target_pairs={{0,4},{4,0},{8,12},{12,8},{16,20},{20,16},{24,28},{28,24},{32,36},... | collective-permute-start | bytes 1474568 | tf_op jit(solution)/shard_map/ppermute | solution.py:304
  169.9 10.7 %all-to-all-start.4 = ((f32[4,96,160]{1,2,0:T(8,128)}), f32[4,96,160]{1,2,0:T(8,128)S(1)}, u32[]{:S(2)}, u32[]{:S(2)}) async-start(f32[4,96,160]{1,2,0:T(8,128)} %copy.62), calls=%async_computation.4 | async-start | bytes 655360 | tf_op jit(solution)/shard_map/all_to_all | solution.py:294
where the time goes:
time: 182 us; the launch traced here: 181 us
  waiting for transfers between devices  55.3 us (30%)
  Pallas kernels  52 us (29%)
  blocking collectives  31.8 us (17%)
  starting transfers between devices  23.6 us (13%)
  local copies, waits for them, and re-layouts  14 us (8%)
  other arithmetic  2.88 us (2%)
    all_to_all x3, waiting for transfers between devices, exchange(): lax.all_to_all(x, axis, split_axis=0, concat_axis=0, tiled=True, axis_ind...  50.8 us
    pallas_call x1, Pallas kernels, attention(): pl.pallas_call(functools.partial(attention_kernel, kv_local, group, log_s...  43.4 us
    all_to_all x2, blocking collectives, exchange(): lax.all_to_all(x, axis, split_axis=0, concat_axis=0, tiled=True, axis_ind...  31.8 us
    all_to_all x3, starting transfers between devices, exchange(): lax.all_to_all(x, axis, split_axis=0, concat_axis=0, tiled=True, axis_ind...  19.3 us
    unnamed x23, local copies, waits for them, and re-layouts  8.38 us
    ppermute x4, waiting for transfers between devices, across(): lax.ppermute(x, axis, [(i, i ^ 1) for i in range(lax.axis_size(axis))])  4.55 us
    ppermute x4, starting transfers between devices, across(): lax.ppermute(x, axis, [(i, i ^ 1) for i in range(lax.axis_size(axis))])  4.35 us
    pallas_call x1, Pallas kernels, pack(): pl.pallas_call(pack_kernel, out_shape=jax.ShapeDtypeStruct((nctx, CAP, 2,...  4.32 us
  transfers between devices with their start and end apart: 7, of which 7 were waited for; matrix products, arithmetic and copies ran while one was open for 2% of the time, Pallas kernels for 29%

commit v1 on v0

--- a/solution.py
+++ b/solution.py
@@ -136,7 +136,7 @@
         grid_spec=pltpu.PrefetchScalarGridSpec(
             num_scalar_prefetch=1,
             grid=(1,),
-            in_specs=[pl.BlockSpec(memory_space=pltpu.HBM)] * 3,
+            in_specs=[pl.BlockSpec(memory_space=pl.ANY)] + [pl.BlockSpec(memory_space=pltpu.HBM)] * 2,
             out_specs=[pl.BlockSpec(memory_space=pltpu.HBM)] * 2,
             scratch_shapes=[
                 pltpu.VMEM((slots, 2, rows, lanes), keys.dtype),
@@ -173,8 +173,12 @@
             [probs, jnp.zeros((probs.shape[0], lanes - width), jnp.float32)], axis=1
         )
     total[r] = total[r] * shrink + part
-    numer[r] = numer[r] * shrink + jnp.dot(
-        probs.astype(jnp.bfloat16), values, preferred_element_type=jnp.float32
+    high = probs.astype(jnp.bfloat16)
+    rest = (probs - high.astype(jnp.float32)).astype(jnp.bfloat16)
+    numer[r] = (
+        numer[r] * shrink
+        + jnp.dot(high, values, preferred_element_type=jnp.float32)
+        + jnp.dot(rest, values, preferred_element_type=jnp.float32)
     )
 
 
@@ -298,6 +302,20 @@
 
 def everywhere(x, axis, groups):
     return exchange(jnp.broadcast_to(x[None], (len(groups[0]), *x.shape)), axis, groups)
+
+
+def around(x, axis):
+    n = lax.axis_size(axis)
+    here = lax.axis_index(axis)
+    turns = [x] + [lax.ppermute(x, axis, [(i, (i + d) % n) for i in range(n)]) for d in range(1, n)]
+    stack = jnp.stack(turns)
+    return jnp.stack(
+        [lax.dynamic_index_in_dim(stack, (here - i) & (n - 1), keepdims=False) for i in range(n)]
+    )
+
+
+def in_order(odd, same, other):
+    return jnp.where(odd, jnp.stack([other, same], axis=1), jnp.stack([same, other], axis=1))
 
 
 def across(x, axis):
@@ -323,29 +341,23 @@
     keys = cache_keys.reshape(blocks, width * kv_local, head_dim)
     values = cache_values.reshape(blocks, width * kv_local, head_dim)
 
-    mine = jnp.concatenate(
-        [
-            queries.reshape(own * heads, head_dim),
-            draft_keys.reshape(own * kv_local, head_dim),
-            draft_values.reshape(own * kv_local, head_dim),
-        ],
-        axis=0,
-    )
+    mine = jnp.concatenate([queries, draft_keys, draft_values], axis=1)
+    mine = mine.reshape(-1, head_dim)
     chips = nctx // 2
-    odd = rank % 2 == 1
+    odd = (rank & 1) == 1
     sides = [[2 * i + side for i in range(chips)] for side in range(2)]
     send = pack(me, move_dst, keys, values, nctx)
     same = everywhere(mine, "ctx", sides)
     same, send = lax.optimization_barrier((same, send))
     recv = exchange(send, "ctx")
     other = across(same, "ctx")
-    shared = jnp.where(odd, jnp.stack([other, same], axis=1), jnp.stack([same, other], axis=1))
-    shared = shared.reshape(nctx, -1, head_dim)
-    cut = own * heads
-    cut2 = cut + own * kv_local
-    q = shared[:, :cut].reshape(requests, drafts * heads, head_dim)
-    dk = shared[:, cut:cut2].reshape(requests, drafts * kv_local, head_dim)
-    dv = shared[:, cut2:].reshape(requests, drafts * kv_local, head_dim)
+    shared = in_order(odd, same, other)
+    shared = shared.reshape(tokens, heads + 2 * kv_local, head_dim)
+    q = shared[:, :heads].reshape(requests, drafts * heads, head_dim)
+    dk = shared[:, heads : heads + kv_local].reshape(requests, drafts * kv_local, head_dim)
+    dv = shared[:, heads + kv_local :].reshape(requests, drafts * kv_local, head_dim)
+    nhead = lax.axis_size("head")
+    weights = around(w_out, "head").reshape(nhead * heads * head_dim, -1)
 
     my_offs = lax.dynamic_slice_in_dim(draft_offs, jnp.minimum(rank, requests - 1), 1)[0]
     offs = jnp.repeat(my_offs, heads)[:, None]
@@ -353,16 +365,17 @@
         me, block_req, block_idx, move_dst, lengths, q, dk, dv, offs, keys, values,
         slots, kv_local, group, log_scale,
     )
-    rows = own * heads
-
-    def halves(x):
-        x = x.reshape(chips, 2, *x.shape[1:])
-        return jnp.where(odd, x[:, 1], x[:, 0]), jnp.where(odd, x[:, 0], x[:, 1])
-
-    kept, given = halves(numer.reshape(nctx, rows, head_dim))
-    kept_notes, given_notes = halves(
-        jnp.swapaxes(stats[:, :2], 0, 1).reshape(2, nctx, rows).swapaxes(0, 1)
-    )
+    each = own * heads // nhead
+
+    def by_target(x):
+        lanes = x.shape[-1]
+        x = x.reshape(nhead, chips, 2, each, lanes)
+        x = jnp.transpose(x, (2, 1, 0, 3, 4)).reshape(2, chips * nhead, each, lanes)
+        return jnp.where(odd, x[1], x[0]), jnp.where(odd, x[0], x[1])
+
+    kept, given = by_target(numer)
+    kept_notes, given_notes = by_target(jnp.swapaxes(stats[:, :2], 1, 2))
+    kept_notes, given_notes = kept_notes.swapaxes(1, 2), given_notes.swapaxes(1, 2)
     taken, taken_notes = across(given, "ctx"), across(given_notes, "ctx")
     pair_top = jnp.maximum(kept_notes[:, 0], taken_notes[:, 0])
     fa = jnp.exp2((kept_notes[:, 0] - pair_top) * log_scale)
@@ -371,32 +384,31 @@
     sums = kept_notes[:, 1] * fa + taken_notes[:, 1] * fb
     high = sums.astype(jnp.bfloat16)
     rest = (sums - high.astype(jnp.float32)).astype(jnp.bfloat16)
-    notes = jnp.stack([pair_top.astype(jnp.bfloat16), high, rest], axis=1)
-    notes = jnp.pad(notes, ((0, 0), (0, 5), (0, head_dim - rows)))
+    notes = jnp.concatenate([pair_top.astype(jnp.bfloat16), high, rest], axis=1)[:, None]
+    notes = jnp.pad(notes, ((0, 0), (0, 1), (0, head_dim - 3 * each)))
     packet = jnp.concatenate([pair, notes], axis=1)
-    packet, recv = lax.optimization_barrier((packet, recv))
-    parts = exchange(packet, "ctx", sides)
+    packet, recv, weights = lax.optimization_barrier((packet, recv, weights))
+    groups = [
+        [(2 * i + side) * nhead + h for i in range(chips) for h in range(nhead)]
+        for side in range(2)
+    ]
+    parts = exchange(packet, ("ctx", "head"), groups)
     count = jnp.sum((move_dst.reshape(nctx, blocks) == rank).astype(jnp.int32), axis=1)
     new_keys, new_values = unpack(count, recv, new_keys, new_values, slots)
-    notes = parts[:, rows : rows + 3, :rows].astype(jnp.float32)
-    top = jnp.max(notes[:, 0], axis=0)
-    factor = jnp.exp2((notes[:, 0] - top) * log_scale)
-    denom = jnp.sum(factor * (notes[:, 1] + notes[:, 2]), axis=0)
-    total = jnp.sum(parts[:, :rows].astype(jnp.float32) * factor[:, :, None], axis=0)
-    attn = (total / denom[:, None]).astype(jnp.bfloat16)
-    same = everywhere(attn.reshape(own, heads * head_dim), "ctx", sides)
+    parts, new_keys, new_values = lax.optimization_barrier((parts, new_keys, new_values))
+    parts = parts.reshape(chips, nhead, each + 2, head_dim)
+    notes = parts[:, :, each, : 3 * each].reshape(chips, nhead, 3, each).astype(jnp.float32)
+    top = jnp.max(notes[:, :, 0], axis=0)
+    factor = jnp.exp2((notes[:, :, 0] - top) * log_scale)
+    denom = jnp.sum(factor * (notes[:, :, 1] + notes[:, :, 2]), axis=0)
+    total = jnp.sum(parts[:, :, :each].astype(jnp.float32) * factor[..., None], axis=0)
+    attn = (total / denom[..., None]).astype(jnp.bfloat16)
+    share = own // nhead
+    line = attn.reshape(nhead, share, heads, head_dim).swapaxes(0, 1).reshape(-1, head_dim)
+    same = everywhere(line, "ctx", sides)
     other = across(same, "ctx")
-
-    def project(x):
-        x = x.reshape(chips * own, heads * head_dim)
-        y = jnp.dot(x, w_out, preferred_element_type=jnp.float32)
-        return y.reshape(chips, own, -1)
-
-    same, other = project(same), project(other)
-    partial = jnp.where(odd, jnp.stack([other, same], axis=1), jnp.stack([same, other], axis=1))
-    nhead = lax.axis_size("head")
-    shares = exchange(partial.reshape(nhead, tokens // nhead, -1), "head")
-    mixed = functools.reduce(jnp.add, [shares[i] for i in range(nhead)]).astype(jnp.bfloat16)
+    full = in_order(odd, same, other).reshape(nctx * share, nhead * heads * head_dim)
+    mixed = jnp.dot(full, weights, preferred_element_type=jnp.float32).astype(jnp.bfloat16)
     shape = (blocks + slots, width, kv_local, head_dim)
     return (mixed, new_keys.reshape(shape), new_values.reshape(shape))
 

time: 182 us -> 177 us (0.973)
  blocking collectives: 31.8 us -> 11.7 us
  starting transfers between devices: 23.6 us -> 37 us
  Pallas kernels: 52 us -> 39.4 us
  local copies, waits for them, and re-layouts: 14 us -> 19.9 us
  other arithmetic: 2.88 us -> 6.75 us
  waiting for transfers between devices: 55.3 us -> 57.8 us
    all_to_all x2 -> x1, blocking collectives: 31.8 us -> 11.7 us  [exchange(): lax.all_to_all(x, axis, split_axis=0, concat_axis=0, tiled=True, axis_ind...]
    ppermute x0 -> x3, waiting for transfers between devices: none -> 16 us  [around(): lax.ppermute(x, axis, [(i, (i + d) % n) for i in range(n)])]
    pallas_call x1, Pallas kernels: 43.4 us -> 30.3 us  [attention(): pl.pallas_call(functools.partial(attention_kernel, kv_local, group, log_s...]
    all_to_all x3, waiting for transfers between devices: 50.8 us -> 38.8 us  [exchange(): lax.all_to_all(x, axis, split_axis=0, concat_axis=0, tiled=True, axis_ind...]
    all_to_all x3, starting transfers between devices: 19.3 us -> 26.6 us  [exchange(): lax.all_to_all(x, axis, split_axis=0, concat_axis=0, tiled=True, axis_ind...]
    ppermute x0 -> x3, starting transfers between devices: none -> 4.45 us  [around(): lax.ppermute(x, axis, [(i, (i + d) % n) for i in range(n)])]
    select_n x3 -> x6, local copies, waits for them, and re-layouts: 1.21 us -> 4.09 us  [the longest x4 2.29 us: by_target(): return (jnp.where(odd, x[1], x[0]), jnp.where(odd, x[0], x[1]))]
    select_n x4, other arithmetic: 0.42 us -> 2.35 us  [the longest x2 1.87 us: by_target(): return (jnp.where(odd, x[1], x[0]), jnp.where(odd, x[0], x[1]))]
  transfers between devices with their start and end apart: 7 -> 10, of which waited for: 7 -> 7; matrix products, arithmetic and copies ran while one was open for 2% -> 7% of each run, Pallas kernels for 29% -> 22%
where the time goes in v1:
time: 177 us; the launch traced here: 176 us
  waiting for transfers between devices  57.8 us (33%)
  Pallas kernels  39.4 us (22%)
  starting transfers between devices  37 us (21%)
  local copies, waits for them, and re-layouts  19.9 us (11%)
  blocking collectives  11.7 us (7%)
  other arithmetic  6.75 us (4%)
  matrix products  2.4 us (1%)
    all_to_all x3, waiting for transfers between devices, exchange(): lax.all_to_all(x, axis, split_axis=0, concat_axis=0, tiled=True, axis_ind...  38.8 us
    pallas_call x1, Pallas kernels, attention(): pl.pallas_call(functools.partial(attention_kernel, kv_local, group, log_s...  30.3 us
    all_to_all x3, starting transfers between devices, exchange(): lax.all_to_all(x, axis, split_axis=0, concat_axis=0, tiled=True, axis_ind...  26.6 us
    ppermute x3, waiting for transfers between devices, around(): lax.ppermute(x, axis, [(i, (i + d) % n) for i in range(n)])  16 us
    all_to_all x1, blocking collectives, exchange(): lax.all_to_all(x, axis, split_axis=0, concat_axis=0, tiled=True, axis_ind...  11.7 us
    unnamed x28, local copies, waits for them, and re-layouts  8.8 us
    ppermute x4, starting transfers between devices, across(): lax.ppermute(x, axis, [(i, i ^ 1) for i in range(lax.axis_size(axis))])  5.94 us
    pallas_call x1, Pallas kernels, unpack(): pl.pallas_call(functools.partial(unpack_kernel, slots), out_shape=(shape,...  5.47 us
  transfers between devices with their start and end apart: 10, of which 7 were waited for; matrix products, arithmetic and copies ran while one was open for 7% of the time, Pallas kernels for 22%

profile of v1, /device:TPU:1, one launch (start us, length us, event | category | flops | bytes accessed | tf_op | source)
XLA Modules:
  0.0 176.0 jit_solution(6845032152660855122)
XLA Ops:
  0.7 0.8 pad_maximum_fusion.1
  1.6 0.9 broadcast_in_dim.26
  2.5 8.4 %all-to-all-start = ((bf16[16,168,128]{2,1,0:T(8,128)(2,1)}), bf16[16,168,128]{2,1,0:T(8,128)(2,1)S(1)}, u32[]{:S(2)}, u32[]{:S(2)}) async-start(bf16[16,168,128]{2,1,0:T(8,128)(2,1)} %broadcast_in_dim.26), calls=%async_computation | async-start | bytes 1376256 | tf_op jit(solution)/shard_map/all_to_all | solution.py:298
  11.0 2.2 %copy-done.2 = bf16[64,128,2,128]{3,2,1,0:T(2,128)(2,1)S(1)} copy-done((bf16[64,128,2,128]{3,2,1,0:T(2,128)(2,1)S(1)}, bf16[64,128,2,128]{3,2,1,0:T(2,128)(2,1)}, u32[]{:S(2)}) %copy-start.2) | copy-done | bytes 4194328
  13.2 2.2 %copy-done.4 = bf16[64,128,2,128]{3,2,1,0:T(2,128)(2,1)S(1)} copy-done((bf16[64,128,2,128]{3,2,1,0:T(2,128)(2,1)S(1)}, bf16[64,128,2,128]{3,2,1,0:T(2,128)(2,1)}, u32[]{:S(2)}) %copy-start.4) | copy-done | bytes 4194328
  15.3 3.7 %pack.1 = bf16[32,2,2,256,128]{4,3,2,1,0:T(8,128)(2,1)} custom-call(s32[1]{0:T(128)} %bitcast.rank_ref, s32[2048]{0:T(1024)S(1)} %copy-done.6, bf16[64,256,128]{2,1,0:T(8,128)(2,1)S(1)} %bitcast.93, bf16[64,256,128]{2,1,0:T(8,128)(2,1)S(1)} %bitcast.95), custom_call_target="tpu_custom_call" | custom-call | bytes 16777216 | tf_op jit(solution)/shard_map/pack/pallas_call | solution.py:59
  19.1 4.0 %all-to-all-done = bf16[16,168,128]{2,1,0:T(8,128)(2,1)S(1)} async-done(((bf16[16,168,128]{2,1,0:T(8,128)(2,1)}), bf16[16,168,128]{2,1,0:T(8,128)(2,1)S(1)}, u32[]{:S(2)}, u32[]{:S(2)}) %all-to-all-start) | async-done | bytes 688160 | tf_op jit(solution)/shard_map/all_to_all | solution.py:298
  23.1 6.7 %all-to-all-start.1 = ((bf16[32,2,2,256,128]{4,3,2,1,0:T(8,128)(2,1)}), bf16[32,2,2,256,128]{4,3,2,1,0:T(8,128)(2,1)}, u32[]{:S(2)}, u32[]{:S(2)}) async-start(bf16[32,2,2,256,128]{4,3,2,1,0:T(8,128)(2,1)} %pack.1), calls=%async_computation.1 | async-start | bytes 16777216 | tf_op jit(solution)/shard_map/all_to_all | solution.py:298
  29.8 1.4 collective-permute-start.3
  31.1 1.5 collective-permute-start.5
  32.6 1.6 collective-permute-start.4
  34.2 1.3 collective-permute-start
  35.5 0.2 dynamic-slice_reduce_fusion
  35.8 6.1 %collective-permute-done.3 = bf16[1280,160]{0,1:T(8,128)(2,1)S(1)} collective-permute-done((bf16[1280,160]{0,1:T(8,128)(2,1)S(1)}, bf16[1280,160]{0,1:T(8,128)(2,1)S(1)}, u32[]{:S(2)}, u32[]{:S(2)}) %collective-permute-start.3) | collective-permute-done | bytes 409632 | tf_op jit(solution)/shard_map/ppermute | solution.py:310
  41.9 9.9 %collective-permute-done.4 = bf16[1280,160]{0,1:T(8,128)(2,1)S(1)} collective-permute-done((bf16[1280,160]{0,1:T(8,128)(2,1)S(1)}, bf16[1280,160]{0,1:T(8,128)(2,1)S(1)}, u32[]{:S(2)}, u32[]{:S(2)}) %collective-permute-start.4) | collective-permute-done | bytes 409632 | tf_op jit(solution)/shard_map/ppermute | solution.py:310
  51.8 0.2 pad_maximum_fusion
  52.0 1.1 constant_dynamic-slice_fusion.3
  53.1 0.3 maximum_select_fusion
  53.4 0.4 select_n.80
  53.8 0.4 reshape.123.q_ref
  54.2 0.4 fusion.8
  54.6 2.2 %copy-done.3 = bf16[64,128,2,128]{3,2,1,0:T(2,128)(2,1)S(1)} copy-done((bf16[64,128,2,128]{3,2,1,0:T(2,128)(2,1)S(1)}, bf16[64,128,2,128]{3,2,1,0:T(2,128)(2,1)}, u32[]{:S(2)}) %copy-start.3) | copy-done | bytes 4194328
  56.8 2.2 %copy-done.5 = bf16[64,128,2,128]{3,2,1,0:T(2,128)(2,1)S(1)} copy-done((bf16[64,128,2,128]{3,2,1,0:T(2,128)(2,1)S(1)}, bf16[64,128,2,128]{3,2,1,0:T(2,128)(2,1)}, u32[]{:S(2)}) %copy-start.5) | copy-done | bytes 4194328
  59.0 30.3 %attention.1 = (f32[24,160,128]{2,1,0:T(8,128)S(1)}, f32[24,8,160]{2,1,0:T(8,128)S(1)}, bf16[96,256,128]{2,1,0:T(8,128)(2,1)}, bf16[96,256,128]{2,1,0:T(8,128)(2,1)}) custom-call(s32[1]{0:T(128)} %bitcast.rank_ref, s32[2048]{0:T(1024)S(1)} %copy-done.7, s32[2048]{0:T(1024)S(1)} %copy-done.8, s32[2048]{0:T(1024)S(1)} %copy-done.6, s32[24]{0:T(128)S(1)} %copy-done.9, ...), custom_call_target="tpu_custom_call" | custom-call | flops 1342177280 | bytes 16777216 | tf_op jit(solution)/shard_map/attention/pallas_call | solution.py:267
  89.3 0.3 reshape.127
  89.7 1.2 collective-permute-start.1
  90.9 1.5 reshape.126
  92.4 1.8 %slice_select_fusion.1 = (f32[1,16,4,30,128]{4,3,0,1,2:T(8,128)S(1)}, f32[1,16,4,30,128]{4,3,0,1,2:T(8,128)S(1)}) fusion(f32[2,16,4,30,128]{4,3,0,1,2:T(8,128)} %bitcast.99, pred[]{:T(512)S(6)} %eq.10), kind=kLoop, calls=%fused_computation.8 | loop fusion | flops 491520 | bytes 3932161 | tf_op jit(solution)/shard_map/jit(_where)/select_n | solution.py:374
  94.2 1.6 copy.81
  95.8 0.2 maximum_bitcast_fusion
  96.1 0.2 copy.93
  96.3 0.6 copy.76
  97.2 1.5 collective-permute-done.2
  98.7 1.8 %add_convert_fusion = bf16[64,30,128]{2,0,1:T(8,128)(2,1)S(1)} fusion(f32[64,30,128]{2,0,1:T(8,128)} %collective-permute-done.2, f32[64,30,128]{2,0,1:T(8,128)S(1)} %bitcast.104, f32[64,30]{0,1:T(8,128)S(1)} %copy.82, f32[64,30]{0,1:T(8,128)S(1)} %copy.80), kind=kLoop, calls=%fused_computation.10 | loop fusion | flops 983040 | bytes 2472960 | tf_op jit(solution)/shard_map/convert_element_type | solution.py:383
  100.6 29.0 %all-to-all-done.1.recv_ref = bf16[32,2,2,256,128]{4,3,2,1,0:T(8,128)(2,1)} async-done(((bf16[32,2,2,256,128]{4,3,2,1,0:T(8,128)(2,1)}), bf16[32,2,2,256,128]{4,3,2,1,0:T(8,128)(2,1)}, u32[]{:S(2)}, u32[]{:S(2)}) %all-to-all-start.1) | async-done | bytes 8388640 | tf_op jit(solution)/shard_map/all_to_all | solution.py:298
  129.5 1.2 copy.84
  130.7 11.5 %all-to-all-start.2 = ((bf16[64,32,128]{2,1,0:T(8,128)(2,1)}), bf16[64,32,128]{2,1,0:T(8,128)(2,1)S(1)}, u32[]{:S(2)}, u32[]{:S(2)}) async-start(bf16[64,32,128]{2,1,0:T(8,128)(2,1)} %copy.84), calls=%async_computation.2 | async-start | bytes 1048576 | tf_op jit(solution)/shard_map/all_to_all | solution.py:298
  142.3 0.6 reduce_sum.29.count_ref
  142.9 5.5 %unpack.1 = (bf16[96,256,128]{2,1,0:T(8,128)(2,1)}, bf16[96,256,128]{2,1,0:T(8,128)(2,1)}) custom-call(s32[32]{0:T(128)} %reduce_sum.29.count_ref, bf16[32,2,2,256,128]{4,3,2,1,0:T(8,128)(2,1)} %all-to-all-done.1.recv_ref, bf16[96,256,128]{2,1,0:T(8,128)(2,1)} %get-tuple-element.23._k, ...), custom_call_target="tpu_custom_call", output_to_operand_aliasing={{0}: (2, {}), {1}: (3, {})} | custom-call | bytes 8388608 | tf_op jit(solution)/shard_map/unpack/pallas_call | solution.py:133
  148.4 5.9 %all-to-all-done.2 = bf16[64,32,128]{2,1,0:T(8,128)(2,1)S(1)} async-done(((bf16[64,32,128]{2,1,0:T(8,128)(2,1)}), bf16[64,32,128]{2,1,0:T(8,128)(2,1)S(1)}, u32[]{:S(2)}, u32[]{:S(2)}) %all-to-all-start.2) | async-done | bytes 524320 | tf_op jit(solution)/shard_map/all_to_all | solution.py:298
  154.7 0.1 copy.89
  154.8 0.3 multiply_reduce_fusion
  155.4 11.7 %all_to_all.20 = bf16[16,120,128]{2,1,0:T(8,128)(2,1)S(1)} all-to-all(bf16[16,120,128]{2,1,0:T(8,128)(2,1)S(1)} %broadcast_in_dim.30), channel_id=1, replica_groups={{0,8,16,24,32,40,48,56,64,72,80,88,96,104,112,120},{4,12,20,28,36,44,52..., dimensions={0} | all-to-all | bytes 983040 | tf_op jit(solution)/shard_map/all_to_all | solution.py:298
  167.1 3.4 %collective-permute-start.6 = (bf16[16,120,128]{2,1,0:T(8,128)(2,1)S(1)}, bf16[16,120,128]{2,1,0:T(8,128)(2,1)S(1)}, u32[]{:S(2)}, u32[]{:S(2)}) collective-permute-start(bf16[16,120,128]{2,1,0:T(8,128)(2,1)S(1)} %all_to_all.20), channel_id=1, source_target_pairs={{0,4},{4,0},{8,12},{12,8},{16,20},{20,16},{24,28},{28,24},{32,36},... | collective-permute-start | bytes 1474568 | tf_op jit(solution)/shard_map/ppermute | solution.py:322
  170.5 1.5 collective-permute-done.6
  172.0 0.2 maximum_select_fusion.1
  172.2 1.4 select_n.96
  173.6 2.4 %convolution_convert_fusion = bf16[96,160]{0,1:T(8,128)(2,1)} fusion(bf16[96,5120]{1,0:T(8,128)(2,1)} %select_n.96, bf16[5120,160]{0,1:T(8,128)(2,1)S(1)} %bitcast.101), kind=kOutput, calls=%fused_computation.3 | convolution fusion | flops 157301760 | bytes 2652160 | tf_op jit(solution)/shard_map/dot_general | solution.py:411
  (58 shorter events, 1.5 us)
Async XLA Ops:
  0.6 34.8 %copy-start = (s32[24,16]{0,1:T(8,128)S(1)}, s32[24,16]{0,1:T(8,128)}, u32[]{:S(2)}) copy-start(s32[24,16]{0,1:T(8,128)} %param.21) | copy-start | bytes 4612
  0.6 10.3 %copy-start.6 = (s32[2048]{0:T(1024)S(1)}, s32[2048]{0:T(1024)}, u32[]{:S(2)}) copy-start(s32[2048]{0:T(1024)} %dst_ref.3) | copy-start | bytes 24580
  2.5 20.6 %all-to-all-start = ((bf16[16,168,128]{2,1,0:T(8,128)(2,1)}), bf16[16,168,128]{2,1,0:T(8,128)(2,1)S(1)}, u32[]{:S(2)}, u32[]{:S(2)}) async-start(bf16[16,168,128]{2,1,0:T(8,128)(2,1)} %broadcast_in_dim.26), calls=%async_computation | async-start | bytes 1376256 | tf_op jit(solution)/shard_map/all_to_all | solution.py:298
  11.0 2.2 %copy-start.2 = (bf16[64,128,2,128]{3,2,1,0:T(2,128)(2,1)S(1)}, bf16[64,128,2,128]{3,2,1,0:T(2,128)(2,1)}, u32[]{:S(2)}) copy-start(bf16[64,128,2,128]{3,2,1,0:T(2,128)(2,1)} %param.14) | copy-start | bytes 12582916
  13.2 2.2 %copy-start.4 = (bf16[64,128,2,128]{3,2,1,0:T(2,128)(2,1)S(1)}, bf16[64,128,2,128]{3,2,1,0:T(2,128)(2,1)}, u32[]{:S(2)}) copy-start(bf16[64,128,2,128]{3,2,1,0:T(2,128)(2,1)} %param.15) | copy-start | bytes 12582916
  19.0 10.7 %copy-start.13 = (bf16[1280,160]{0,1:T(8,128)(2,1)S(1)}, bf16[1280,160]{0,1:T(8,128)(2,1)}, u32[]{:S(2)}) copy-start(bf16[1280,160]{0,1:T(8,128)(2,1)} %param.16) | copy-start | bytes 1228804
  23.1 106.4 %all-to-all-start.1 = ((bf16[32,2,2,256,128]{4,3,2,1,0:T(8,128)(2,1)}), bf16[32,2,2,256,128]{4,3,2,1,0:T(8,128)(2,1)}, u32[]{:S(2)}, u32[]{:S(2)}) async-start(bf16[32,2,2,256,128]{4,3,2,1,0:T(8,128)(2,1)} %pack.1), calls=%async_computation.1 | async-start | bytes 16777216 | tf_op jit(solution)/shard_map/all_to_all | solution.py:298
  29.8 12.1 %collective-permute-start.3 = (bf16[1280,160]{0,1:T(8,128)(2,1)S(1)}, bf16[1280,160]{0,1:T(8,128)(2,1)S(1)}, u32[]{:S(2)}, u32[]{:S(2)}) collective-permute-start(bf16[1280,160]{0,1:T(8,128)(2,1)S(1)} %copy-done.13), channel_id=1, source_target_pairs={{0,1},{1,2},{2,3},{3,0},{4,5},{5,6},{6,7},{7,4},{8,9},{9,10},{10,1... | collective-permute-start | bytes 1228808 | tf_op jit(solution)/shard_map/ppermute | solution.py:310
  31.1 10.8 %collective-permute-start.5 = (bf16[1280,160]{0,1:T(8,128)(2,1)S(1)}, bf16[1280,160]{0,1:T(8,128)(2,1)S(1)}, u32[]{:S(2)}, u32[]{:S(2)}) collective-permute-start(bf16[1280,160]{0,1:T(8,128)(2,1)S(1)} %copy-done.13), channel_id=1, source_target_pairs={{0,3},{1,0},{2,1},{3,2},{4,7},{5,4},{6,5},{7,6},{8,11},{9,8},{10,9... | collective-permute-start | bytes 1228808 | tf_op jit(solution)/shard_map/ppermute | solution.py:310
  32.6 19.1 %collective-permute-start.4 = (bf16[1280,160]{0,1:T(8,128)(2,1)S(1)}, bf16[1280,160]{0,1:T(8,128)(2,1)S(1)}, u32[]{:S(2)}, u32[]{:S(2)}) collective-permute-start(bf16[1280,160]{0,1:T(8,128)(2,1)S(1)} %copy-done.13), channel_id=1, source_target_pairs={{0,2},{1,3},{2,0},{3,1},{4,6},{5,7},{6,4},{7,5},{8,10},{9,11},{10,... | collective-permute-start | bytes 1228808 | tf_op jit(solution)/shard_map/ppermute | solution.py:310
  34.2 18.9 %collective-permute-start = (bf16[16,168,128]{2,1,0:T(8,128)(2,1)S(1)}, bf16[16,168,128]{2,1,0:T(8,128)(2,1)S(1)}, u32[]{:S(2)}, u32[]{:S(2)}) collective-permute-start(bf16[16,168,128]{2,1,0:T(8,128)(2,1)S(1)} %all-to-all-done), channel_id=1, source_target_pairs={{0,4},{4,0},{8,12},{12,8},{16,20},{20,16},{24,28},{28,24},{32,36},... | collective-permute-start | bytes 2064392 | tf_op jit(solution)/shard_map/ppermute | solution.py:322
  53.8 0.8 copy-start.7
  53.8 0.8 copy-start.8
  53.8 0.8 copy-start.9
  54.6 2.2 %copy-start.3 = (bf16[64,128,2,128]{3,2,1,0:T(2,128)(2,1)S(1)}, bf16[64,128,2,128]{3,2,1,0:T(2,128)(2,1)}, u32[]{:S(2)}) copy-start(bf16[64,128,2,128]{3,2,1,0:T(2,128)(2,1)} %param.14) | copy-start | bytes 12582916
  56.8 2.2 %copy-start.5 = (bf16[64,128,2,128]{3,2,1,0:T(2,128)(2,1)S(1)}, bf16[64,128,2,128]{3,2,1,0:T(2,128)(2,1)}, u32[]{:S(2)}) copy-start(bf16[64,128,2,128]{3,2,1,0:T(2,128)(2,1)} %param.15) | copy-start | bytes 12582916
  89.7 7.2 %collective-permute-start.1 = (f32[64,2,30]{2,0,1:T(8,128)S(1)}, f32[64,2,30]{2,0,1:T(8,128)S(1)}, u32[]{:S(2)}, u32[]{:S(2)}) collective-permute-start(f32[64,2,30]{2,0,1:T(8,128)S(1)} %bitcast.122), channel_id=1, source_target_pairs={{0,4},{4,0},{8,12},{12,8},{16,20},{20,16},{24,28},{28,24},{32,36},... | collective-permute-start | bytes 46088 | tf_op jit(solution)/shard_map/ppermute | solution.py:322
  94.2 1.6 copy-start.10
  94.2 1.6 copy-start.11
  94.2 1.6 copy-start.12
  95.8 2.9 %collective-permute-start.2 = (f32[64,30,128]{2,0,1:T(8,128)}, f32[64,30,128]{2,0,1:T(8,128)}, u32[]{:S(2)}, u32[]{:S(2)}) collective-permute-start(f32[64,30,128]{2,0,1:T(8,128)} %bitcast.17), channel_id=1, source_target_pairs={{0,4},{4,0},{8,12},{12,8},{16,20},{20,16},{24,28},{28,24},{32,36},... | collective-permute-start | bytes 2949128 | tf_op jit(solution)/shard_map/ppermute | solution.py:322
  130.7 23.6 %all-to-all-start.2 = ((bf16[64,32,128]{2,1,0:T(8,128)(2,1)}), bf16[64,32,128]{2,1,0:T(8,128)(2,1)S(1)}, u32[]{:S(2)}, u32[]{:S(2)}) async-start(bf16[64,32,128]{2,1,0:T(8,128)(2,1)} %copy.84), calls=%async_computation.2 | async-start | bytes 1048576 | tf_op jit(solution)/shard_map/all_to_all | solution.py:298
  167.1 4.9 %collective-permute-start.6 = (bf16[16,120,128]{2,1,0:T(8,128)(2,1)S(1)}, bf16[16,120,128]{2,1,0:T(8,128)(2,1)S(1)}, u32[]{:S(2)}, u32[]{:S(2)}) collective-permute-start(bf16[16,120,128]{2,1,0:T(8,128)(2,1)S(1)} %all_to_all.20), channel_id=1, source_target_pairs={{0,4},{4,0},{8,12},{12,8},{16,20},{20,16},{24,28},{28,24},{32,36},... | collective-permute-start | bytes 1474568 | tf_op jit(solution)/shard_map/ppermute | solution.py:322
  172.2 3.8 %copy-start.1 = (s32[24,16]{0,1:T(8,128)S(1)}, s32[24,16]{0,1:T(8,128)}, u32[]{:S(2)}) copy-start(s32[24,16]{0,1:T(8,128)} %param.21) | copy-start | bytes 4612

commit v2 on v1

--- a/solution.py
+++ b/solution.py
@@ -13,7 +13,7 @@
 LOW = -1e30
 
 
-def pack_kernel(rank_ref, dst_ref, k_ref, v_ref, send_ref, used, sems):
+def pack_kernel(rank_ref, dst_ref, at_ref, k_ref, v_ref, send_ref, used, sems):
     blocks = k_ref.shape[0]
     base = rank_ref[0] * blocks
 
@@ -25,8 +25,8 @@
 
     def copies(b, dst, place):
         return (
-            pltpu.make_async_copy(k_ref.at[b], send_ref.at[dst, place, 0], sems.at[b, 0]),
-            pltpu.make_async_copy(v_ref.at[b], send_ref.at[dst, place, 1], sems.at[b, 1]),
+            pltpu.make_async_copy(k_ref.at[b], send_ref.at[(dst * CAP + place) * 2], sems.at[b, 0]),
+            pltpu.make_async_copy(v_ref.at[b], send_ref.at[(dst * CAP + place) * 2 + 1], sems.at[b, 1]),
         )
 
     def start(b, carry):
@@ -36,7 +36,7 @@
         def _():
             place = jnp.minimum(used[dst], CAP - 1)
             used[dst] = place + 1
-            for c in copies(b, dst, place):
+            for c in copies(b, at_ref[dst], place):
                 c.start()
 
         return carry
@@ -54,13 +54,13 @@
     lax.fori_loop(0, blocks, finish, 0)
 
 
-def pack(rank, move_dst, keys, values, nctx):
+def pack(rank, move_dst, at, keys, values, nctx):
     blocks, rows, lanes = keys.shape
     return pl.pallas_call(
         pack_kernel,
-        out_shape=jax.ShapeDtypeStruct((nctx, CAP, 2, rows, lanes), keys.dtype),
+        out_shape=jax.ShapeDtypeStruct((nctx * CAP * 2, rows, lanes), keys.dtype),
         grid_spec=pltpu.PrefetchScalarGridSpec(
-            num_scalar_prefetch=2,
+            num_scalar_prefetch=3,
             grid=(1,),
             in_specs=[pl.BlockSpec((blocks, rows, lanes), lambda i, *_: (0, 0, 0))] * 2,
             out_specs=pl.BlockSpec(memory_space=pltpu.HBM),
@@ -74,17 +74,17 @@
             flops=0, bytes_accessed=4 * blocks * rows * lanes * 2, transcendentals=0
         ),
         name="pack",
-    )(rank, move_dst, keys, values)
-
-
-def unpack_kernel(slots, count_ref, recv_ref, _k, _v, k_out, v_out, stage, loads, stores):
+    )(rank, move_dst, at, keys, values)
+
+
+def unpack_kernel(slots, count_ref, at_ref, recv_ref, _k, _v, k_out, v_out, stage, loads, stores):
     nctx = count_ref.shape[0]
     first = k_out.shape[0] - slots
     outs = (k_out, v_out)
 
     def load(row, place, slot, i):
         return pltpu.make_async_copy(
-            recv_ref.at[row, place, i], stage.at[slot, i], loads.at[slot, i]
+            recv_ref.at[(row * CAP + place) * 2 + i], stage.at[slot, i], loads.at[slot, i]
         )
 
     def store(slot, i):
@@ -97,7 +97,7 @@
             @pl.when((count > place) & (slot + place < slots))
             def _():
                 for i in range(2):
-                    load(s, place, slot + place, i).start()
+                    load(at_ref[s], place, slot + place, i).start()
 
         return slot + count
 
@@ -127,14 +127,14 @@
     lax.fori_loop(0, slots, finish, 0)
 
 
-def unpack(count, recv, keys, values, slots):
+def unpack(count, at, recv, keys, values, slots):
     rows, lanes = keys.shape[1:]
     shape = jax.ShapeDtypeStruct(keys.shape, keys.dtype)
     return pl.pallas_call(
         functools.partial(unpack_kernel, slots),
         out_shape=(shape, shape),
         grid_spec=pltpu.PrefetchScalarGridSpec(
-            num_scalar_prefetch=1,
+            num_scalar_prefetch=2,
             grid=(1,),
             in_specs=[pl.BlockSpec(memory_space=pl.ANY)] + [pl.BlockSpec(memory_space=pltpu.HBM)] * 2,
             out_specs=[pl.BlockSpec(memory_space=pltpu.HBM)] * 2,
@@ -144,12 +144,12 @@
                 pltpu.SemaphoreType.DMA((slots, 2)),
             ],
         ),
-        input_output_aliases={2: 0, 3: 1},
+        input_output_aliases={3: 0, 4: 1},
         cost_estimate=pl.CostEstimate(
             flops=0, bytes_accessed=8 * slots * rows * lanes, transcendentals=0
         ),
         name="unpack",
-    )(count, recv, keys, values)
+    )(count, at, recv, keys, values)
 
 
 def attend(q, keys, values, column, limit, top, total, numer, r, log_scale):
@@ -294,6 +294,16 @@
     )(rank, block_req, block_idx, move_dst, lengths, q, dk, dv, offs, keys, values)
 
 
+def settle_kernel(x_ref, out_ref):
+    out_ref[...] = x_ref[...]
+
+
+def settle(x):
+    return pl.pallas_call(
+        settle_kernel, out_shape=jax.ShapeDtypeStruct(x.shape, x.dtype), name="settle"
+    )(x)
+
+
 def exchange(x, axis, groups=None):
     return lax.all_to_all(
         x, axis, split_axis=0, concat_axis=0, tiled=True, axis_index_groups=groups
@@ -346,10 +356,12 @@
     chips = nctx // 2
     odd = (rank & 1) == 1
     sides = [[2 * i + side for i in range(chips)] for side in range(2)]
-    send = pack(me, move_dst, keys, values, nctx)
+    order = [(d + x) % 4 * 8 + x * 2 + c for d in range(4) for x in range(4) for c in range(2)]
+    at = jnp.asarray([order.index(i) for i in range(nctx)], jnp.int32)
+    send = pack(me, move_dst, at, keys, values, nctx)
     same = everywhere(mine, "ctx", sides)
     same, send = lax.optimization_barrier((same, send))
-    recv = exchange(send, "ctx")
+    recv = exchange(send, "ctx", [order])
     other = across(same, "ctx")
     shared = in_order(odd, same, other)
     shared = shared.reshape(tokens, heads + 2 * kv_local, head_dim)
@@ -387,6 +399,7 @@
     notes = jnp.concatenate([pair_top.astype(jnp.bfloat16), high, rest], axis=1)[:, None]
     notes = jnp.pad(notes, ((0, 0), (0, 1), (0, head_dim - 3 * each)))
     packet = jnp.concatenate([pair, notes], axis=1)
+    packet = settle(packet)
     packet, recv, weights = lax.optimization_barrier((packet, recv, weights))
     groups = [
         [(2 * i + side) * nhead + h for i in range(chips) for h in range(nhead)]
@@ -394,7 +407,7 @@
     ]
     parts = exchange(packet, ("ctx", "head"), groups)
     count = jnp.sum((move_dst.reshape(nctx, blocks) == rank).astype(jnp.int32), axis=1)
-    new_keys, new_values = unpack(count, recv, new_keys, new_values, slots)
+    new_keys, new_values = unpack(count, at, recv, new_keys, new_values, slots)
     parts, new_keys, new_values = lax.optimization_barrier((parts, new_keys, new_values))
     parts = parts.reshape(chips, nhead, each + 2, head_dim)
     notes = parts[:, :, each, : 3 * each].reshape(chips, nhead, 3, each).astype(jnp.float32)
@@ -407,8 +420,13 @@
     line = attn.reshape(nhead, share, heads, head_dim).swapaxes(0, 1).reshape(-1, head_dim)
     same = everywhere(line, "ctx", sides)
     other = across(same, "ctx")
-    full = in_order(odd, same, other).reshape(nctx * share, nhead * heads * head_dim)
-    mixed = jnp.dot(full, weights, preferred_element_type=jnp.float32).astype(jnp.bfloat16)
+
+    def project(x):
+        x = x.reshape(chips * share, nhead * heads * head_dim)
+        y = jnp.dot(x, weights, preferred_element_type=jnp.float32).astype(jnp.bfloat16)
+        return y.reshape(chips, share, -1)
+
+    mixed = in_order(odd, project(same), project(other)).reshape(nctx * share, -1)
     shape = (blocks + slots, width, kv_local, head_dim)
     return (mixed, new_keys.reshape(shape), new_values.reshape(shape))
 

time: 177 us -> 172 us (0.972)
  waiting for transfers between devices: 57.8 us -> 38.7 us
  starting transfers between devices: 37 us -> 50.3 us
  Pallas kernels: 39.4 us -> 43.3 us
  local copies, waits for them, and re-layouts: 19.9 us -> 17.4 us
    all_to_all x3, waiting for transfers between devices: 38.8 us -> 20.8 us  [exchange(): lax.all_to_all(x, axis, split_axis=0, concat_axis=0, tiled=True, axis_ind...]
    ppermute x4, starting transfers between devices: 5.94 us -> 20.4 us  [across(): lax.ppermute(x, axis, [(i, i ^ 1) for i in range(lax.axis_size(axis))])]
    pallas_call x1, Pallas kernels: 30.3 us -> 32.3 us  [attention(): pl.pallas_call(functools.partial(attention_kernel, kv_local, group, log_s...]
    pallas_call x1 -> x2, Pallas kernels: 3.69 us -> 5.5 us  [the longest x1 3.63 us: pack(): pl.pallas_call(pack_kernel, out_shape=jax.ShapeDtypeStruct((nctx * CAP *...]
    unnamed x28 -> x31, local copies, waits for them, and re-layouts: 8.8 us -> 10 us
  transfers between devices with their start and end apart: 10 -> 10, of which waited for: 7 -> 7; matrix products, arithmetic and copies ran while one was open for 7% -> 7% of each run, Pallas kernels for 22% -> 25%
where the time goes in v2:
time: 172 us; the launch traced here: 171 us
  starting transfers between devices  50.3 us (29%)
  Pallas kernels  43.3 us (25%)
  waiting for transfers between devices  38.7 us (23%)
  local copies, waits for them, and re-layouts  17.4 us (10%)
  blocking collectives  11.9 us (7%)
  other arithmetic  7.21 us (4%)
    pallas_call x1, Pallas kernels, attention(): pl.pallas_call(functools.partial(attention_kernel, kv_local, group, log_s...  32.3 us
    all_to_all x3, starting transfers between devices, exchange(): lax.all_to_all(x, axis, split_axis=0, concat_axis=0, tiled=True, axis_ind...  25.4 us
    all_to_all x3, waiting for transfers between devices, exchange(): lax.all_to_all(x, axis, split_axis=0, concat_axis=0, tiled=True, axis_ind...  20.8 us
    ppermute x4, starting transfers between devices, across(): lax.ppermute(x, axis, [(i, i ^ 1) for i in range(lax.axis_size(axis))])  20.4 us
    ppermute x3, waiting for transfers between devices, around(): lax.ppermute(x, axis, [(i, (i + d) % n) for i in range(n)])  16 us
    all_to_all x1, blocking collectives, exchange(): lax.all_to_all(x, axis, split_axis=0, concat_axis=0, tiled=True, axis_ind...  11.9 us
    unnamed x31, local copies, waits for them, and re-layouts  10 us
    pallas_call x1, Pallas kernels, unpack(): pl.pallas_call(functools.partial(unpack_kernel, slots), out_shape=(shape,...  5.56 us
  transfers between devices with their start and end apart: 10, of which 7 were waited for; matrix products, arithmetic and copies ran while one was open for 7% of the time, Pallas kernels for 25%

profile of v2, /device:TPU:1, one launch (start us, length us, event | category | flops | bytes accessed | tf_op | source)
XLA Modules:
  0.0 171.2 jit_solution(4808408870500447274)
XLA Ops:
  0.7 0.8 pad_maximum_fusion.1
  1.6 0.9 broadcast_in_dim.26
  2.5 8.4 %all-to-all-start = ((bf16[16,168,128]{2,1,0:T(8,128)(2,1)}), bf16[16,168,128]{2,1,0:T(8,128)(2,1)S(1)}, u32[]{:S(2)}, u32[]{:S(2)}) async-start(bf16[16,168,128]{2,1,0:T(8,128)(2,1)} %broadcast_in_dim.26), calls=%async_computation | async-start | bytes 1376256 | tf_op jit(solution)/shard_map/all_to_all | solution.py:308
  11.0 2.2 %copy-done.2 = bf16[64,128,2,128]{3,2,1,0:T(2,128)(2,1)S(1)} copy-done((bf16[64,128,2,128]{3,2,1,0:T(2,128)(2,1)S(1)}, bf16[64,128,2,128]{3,2,1,0:T(2,128)(2,1)}, u32[]{:S(2)}) %copy-start.2) | copy-done | bytes 4194328
  13.2 2.2 %copy-done.4 = bf16[64,128,2,128]{3,2,1,0:T(2,128)(2,1)S(1)} copy-done((bf16[64,128,2,128]{3,2,1,0:T(2,128)(2,1)S(1)}, bf16[64,128,2,128]{3,2,1,0:T(2,128)(2,1)}, u32[]{:S(2)}) %copy-start.4) | copy-done | bytes 4194328
  15.4 3.6 %pack.1 = bf16[128,256,128]{2,1,0:T(8,128)(2,1)} custom-call(s32[1]{0:T(128)} %bitcast.rank_ref, s32[2048]{0:T(1024)S(1)} %copy-done.6, s32[32]{0:T(128)S(1)} %copy-done.9, bf16[64,256,128]{2,1,0:T(8,128)(2,1)S(1)} %bitcast.96, bf16[64,256,128]{2,1,0:T(8,128)(2,1)S(1)} %bitcast.98), custom_call_target="tpu_custom_call" | custom-call | bytes 16777216 | tf_op jit(solution)/shard_map/pack/pallas_call | solution.py:59
  19.0 4.1 %all-to-all-done = bf16[16,168,128]{2,1,0:T(8,128)(2,1)S(1)} async-done(((bf16[16,168,128]{2,1,0:T(8,128)(2,1)}), bf16[16,168,128]{2,1,0:T(8,128)(2,1)S(1)}, u32[]{:S(2)}, u32[]{:S(2)}) %all-to-all-start) | async-done | bytes 688160 | tf_op jit(solution)/shard_map/all_to_all | solution.py:308
  23.1 6.7 %all-to-all-start.1 = ((bf16[128,256,128]{2,1,0:T(8,128)(2,1)}), bf16[128,256,128]{2,1,0:T(8,128)(2,1)}, u32[]{:S(2)}, u32[]{:S(2)}) async-start(bf16[128,256,128]{2,1,0:T(8,128)(2,1)} %pack.1), calls=%async_computation.1 | async-start | bytes 16777216 | tf_op jit(solution)/shard_map/all_to_all | solution.py:308
  29.8 1.4 collective-permute-start.3
  31.1 1.5 collective-permute-start.5
  32.7 1.6 collective-permute-start.4
  34.2 1.3 collective-permute-start
  35.8 6.1 %collective-permute-done.3 = bf16[1280,160]{0,1:T(8,128)(2,1)S(1)} collective-permute-done((bf16[1280,160]{0,1:T(8,128)(2,1)S(1)}, bf16[1280,160]{0,1:T(8,128)(2,1)S(1)}, u32[]{:S(2)}, u32[]{:S(2)}) %collective-permute-start.3) | collective-permute-done | bytes 409632 | tf_op jit(solution)/shard_map/ppermute | solution.py:320
  41.9 9.9 %collective-permute-done.4 = bf16[1280,160]{0,1:T(8,128)(2,1)S(1)} collective-permute-done((bf16[1280,160]{0,1:T(8,128)(2,1)S(1)}, bf16[1280,160]{0,1:T(8,128)(2,1)S(1)}, u32[]{:S(2)}, u32[]{:S(2)}) %collective-permute-start.4) | collective-permute-done | bytes 409632 | tf_op jit(solution)/shard_map/ppermute | solution.py:320
  51.8 0.2 pad_maximum_fusion
  52.0 1.1 constant_dynamic-slice_fusion.3
  53.1 0.3 maximum_select_fusion
  53.4 0.4 select_n.80
  53.8 0.4 reshape.129.q_ref
  54.2 0.4 fusion.10
  54.6 2.2 %copy-done.3 = bf16[64,128,2,128]{3,2,1,0:T(2,128)(2,1)S(1)} copy-done((bf16[64,128,2,128]{3,2,1,0:T(2,128)(2,1)S(1)}, bf16[64,128,2,128]{3,2,1,0:T(2,128)(2,1)}, u32[]{:S(2)}) %copy-start.3) | copy-done | bytes 4194328
  56.8 2.2 %copy-done.5 = bf16[64,128,2,128]{3,2,1,0:T(2,128)(2,1)S(1)} copy-done((bf16[64,128,2,128]{3,2,1,0:T(2,128)(2,1)S(1)}, bf16[64,128,2,128]{3,2,1,0:T(2,128)(2,1)}, u32[]{:S(2)}) %copy-start.5) | copy-done | bytes 4194328
  59.0 32.3 %attention.1 = (f32[24,160,128]{2,1,0:T(8,128)S(1)}, f32[24,8,160]{2,1,0:T(8,128)S(1)}, bf16[96,256,128]{2,1,0:T(8,128)(2,1)}, bf16[96,256,128]{2,1,0:T(8,128)(2,1)}) custom-call(s32[1]{0:T(128)} %bitcast.rank_ref, s32[2048]{0:T(1024)S(1)} %copy-done.7, s32[2048]{0:T(1024)S(1)} %copy-done.8, s32[2048]{0:T(1024)S(1)} %copy-done.6, s32[24]{0:T(128)S(1)} %copy-done.10, ...), custom_call_target="tpu_custom_call" | custom-call | flops 1342177280 | bytes 16777216 | tf_op jit(solution)/shard_map/attention/pallas_call | solution.py:267
  91.3 0.3 reshape.133
  91.7 16.1 %collective-permute-start.1 = (f32[64,2,30]{2,0,1:T(8,128)S(1)}, f32[64,2,30]{2,0,1:T(8,128)S(1)}, u32[]{:S(2)}, u32[]{:S(2)}) collective-permute-start(f32[64,2,30]{2,0,1:T(8,128)S(1)} %bitcast.124), channel_id=1, source_target_pairs={{0,4},{4,0},{8,12},{12,8},{16,20},{20,16},{24,28},{28,24},{32,36},... | collective-permute-start | bytes 46088 | tf_op jit(solution)/shard_map/ppermute | solution.py:332
  107.9 1.5 reshape.132
  109.3 1.8 %slice_select_fusion = (f32[1,16,4,30,128]{4,3,0,1,2:T(8,128)S(1)}, f32[1,16,4,30,128]{4,3,0,1,2:T(8,128)S(1)}) fusion(f32[2,16,4,30,128]{4,3,0,1,2:T(8,128)} %bitcast.104, pred[]{:T(512)S(6)} %eq.10), kind=kLoop, calls=%fused_computation.12 | loop fusion | flops 491520 | bytes 3932161 | tf_op jit(solution)/shard_map/jit(_where)/select_n | solution.py:386
  111.1 0.6 copy.86
  111.9 0.2 copy-done.11
  112.4 0.2 maximum_bitcast_fusion
  113.1 1.4 collective-permute-done.2
  114.4 1.5 fusion.1
  115.9 0.9 fusion.3.x_ref
  116.9 1.9 %settle.1 = bf16[64,32,128]{2,1,0:T(8,128)(2,1)} custom-call(bf16[64,32,128]{2,1,0:T(8,128)(2,1)} %fusion.3.x_ref), custom_call_target="tpu_custom_call" | custom-call | tf_op jit(solution)/shard_map/settle/pallas_call | solution.py:302
  118.7 10.5 %all-to-all-done.1.recv_ref = bf16[128,256,128]{2,1,0:T(8,128)(2,1)} async-done(((bf16[128,256,128]{2,1,0:T(8,128)(2,1)}), bf16[128,256,128]{2,1,0:T(8,128)(2,1)}, u32[]{:S(2)}, u32[]{:S(2)}) %all-to-all-start.1) | async-done | bytes 8388640 | tf_op jit(solution)/shard_map/all_to_all | solution.py:308
  129.2 10.3 %all-to-all-start.2 = ((bf16[64,32,128]{2,1,0:T(8,128)(2,1)}), bf16[64,32,128]{2,1,0:T(8,128)(2,1)S(1)}, u32[]{:S(2)}, u32[]{:S(2)}) async-start(bf16[64,32,128]{2,1,0:T(8,128)(2,1)} %settle.1), calls=%async_computation.2 | async-start | bytes 1048576 | tf_op jit(solution)/shard_map/all_to_all | solution.py:308
  139.6 0.6 reduce_sum.29.count_ref
  140.2 5.6 %unpack.1 = (bf16[96,256,128]{2,1,0:T(8,128)(2,1)}, bf16[96,256,128]{2,1,0:T(8,128)(2,1)}) custom-call(s32[32]{0:T(128)} %reduce_sum.29.count_ref, s32[32]{0:T(128)} %constant.53.clone.at_ref, bf16[128,256,128]{2,1,0:T(8,128)(2,1)} %all-to-all-done.1.recv_ref, ...), custom_call_target="tpu_custom_call", output_to_operand_aliasing={{0}: (3, {}), {1}: (4, {})} | custom-call | bytes 8388608 | tf_op jit(solution)/shard_map/unpack/pallas_call | solution.py:133
  145.8 6.2 %all-to-all-done.2 = bf16[64,32,128]{2,1,0:T(8,128)(2,1)S(1)} async-done(((bf16[64,32,128]{2,1,0:T(8,128)(2,1)}), bf16[64,32,128]{2,1,0:T(8,128)(2,1)S(1)}, u32[]{:S(2)}, u32[]{:S(2)}) %all-to-all-start.2) | async-done | bytes 524320 | tf_op jit(solution)/shard_map/all_to_all | solution.py:308
  152.6 0.3 multiply_reduce_fusion
  153.2 11.9 %all_to_all.20 = bf16[16,120,128]{2,1,0:T(8,128)(2,1)S(1)} all-to-all(bf16[16,120,128]{2,1,0:T(8,128)(2,1)S(1)} %broadcast_in_dim.30), channel_id=1, replica_groups={{0,8,16,24,32,40,48,56,64,72,80,88,96,104,112,120},{4,12,20,28,36,44,52..., dimensions={0} | all-to-all | bytes 983040 | tf_op jit(solution)/shard_map/all_to_all | solution.py:308
  165.0 2.9 %collective-permute-start.6 = (bf16[16,120,128]{2,1,0:T(8,128)(2,1)S(1)}, bf16[16,120,128]{2,1,0:T(8,128)(2,1)S(1)}, u32[]{:S(2)}, u32[]{:S(2)}) collective-permute-start(bf16[16,120,128]{2,1,0:T(8,128)(2,1)S(1)} %all_to_all.20), channel_id=1, source_target_pairs={{0,4},{4,0},{8,12},{12,8},{16,20},{20,16},{24,28},{28,24},{32,36},... | collective-permute-start | bytes 1474568 | tf_op jit(solution)/shard_map/ppermute | solution.py:332
  168.0 0.2 reshape.137
  168.2 0.6 convolution_convert_fusion
  168.9 0.6 collective-permute-done.6
  169.5 0.2 reshape.136
  169.7 0.6 convolution_convert_fusion.1
  170.5 0.7 copy.97
  (66 shorter events, 2.4 us)
Async XLA Ops:
  0.6 34.9 %copy-start = (s32[24,16]{0,1:T(8,128)S(1)}, s32[24,16]{0,1:T(8,128)}, u32[]{:S(2)}) copy-start(s32[24,16]{0,1:T(8,128)} %param.22) | copy-start | bytes 4612
  0.6 10.3 %copy-start.9 = (s32[32]{0:T(128)S(1)}, s32[32]{0:T(128)}, u32[]{:S(2)}) copy-start(s32[32]{0:T(128)} %constant.53.clone.at_ref) | copy-start | bytes 388
  0.7 10.3 %copy-start.6 = (s32[2048]{0:T(1024)S(1)}, s32[2048]{0:T(1024)}, u32[]{:S(2)}) copy-start(s32[2048]{0:T(1024)} %dst_ref.3) | copy-start | bytes 24580
  2.5 20.6 %all-to-all-start = ((bf16[16,168,128]{2,1,0:T(8,128)(2,1)}), bf16[16,168,128]{2,1,0:T(8,128)(2,1)S(1)}, u32[]{:S(2)}, u32[]{:S(2)}) async-start(bf16[16,168,128]{2,1,0:T(8,128)(2,1)} %broadcast_in_dim.26), calls=%async_computation | async-start | bytes 1376256 | tf_op jit(solution)/shard_map/all_to_all | solution.py:308
  11.0 2.2 %copy-start.2 = (bf16[64,128,2,128]{3,2,1,0:T(2,128)(2,1)S(1)}, bf16[64,128,2,128]{3,2,1,0:T(2,128)(2,1)}, u32[]{:S(2)}) copy-start(bf16[64,128,2,128]{3,2,1,0:T(2,128)(2,1)} %param.15) | copy-start | bytes 12582916
  13.2 2.2 %copy-start.4 = (bf16[64,128,2,128]{3,2,1,0:T(2,128)(2,1)S(1)}, bf16[64,128,2,128]{3,2,1,0:T(2,128)(2,1)}, u32[]{:S(2)}) copy-start(bf16[64,128,2,128]{3,2,1,0:T(2,128)(2,1)} %param.16) | copy-start | bytes 12582916
  19.0 10.8 %copy-start.14 = (bf16[1280,160]{0,1:T(8,128)(2,1)S(1)}, bf16[1280,160]{0,1:T(8,128)(2,1)}, u32[]{:S(2)}) copy-start(bf16[1280,160]{0,1:T(8,128)(2,1)} %param.17) | copy-start | bytes 1228804
  23.1 106.1 %all-to-all-start.1 = ((bf16[128,256,128]{2,1,0:T(8,128)(2,1)}), bf16[128,256,128]{2,1,0:T(8,128)(2,1)}, u32[]{:S(2)}, u32[]{:S(2)}) async-start(bf16[128,256,128]{2,1,0:T(8,128)(2,1)} %pack.1), calls=%async_computation.1 | async-start | bytes 16777216 | tf_op jit(solution)/shard_map/all_to_all | solution.py:308
  29.8 12.1 %collective-permute-start.3 = (bf16[1280,160]{0,1:T(8,128)(2,1)S(1)}, bf16[1280,160]{0,1:T(8,128)(2,1)S(1)}, u32[]{:S(2)}, u32[]{:S(2)}) collective-permute-start(bf16[1280,160]{0,1:T(8,128)(2,1)S(1)} %copy-done.14), channel_id=1, source_target_pairs={{0,1},{1,2},{2,3},{3,0},{4,5},{5,6},{6,7},{7,4},{8,9},{9,10},{10,1... | collective-permute-start | bytes 1228808 | tf_op jit(solution)/shard_map/ppermute | solution.py:320
  31.1 10.8 %collective-permute-start.5 = (bf16[1280,160]{0,1:T(8,128)(2,1)S(1)}, bf16[1280,160]{0,1:T(8,128)(2,1)S(1)}, u32[]{:S(2)}, u32[]{:S(2)}) collective-permute-start(bf16[1280,160]{0,1:T(8,128)(2,1)S(1)} %copy-done.14), channel_id=1, source_target_pairs={{0,3},{1,0},{2,1},{3,2},{4,7},{5,4},{6,5},{7,6},{8,11},{9,8},{10,9... | collective-permute-start | bytes 1228808 | tf_op jit(solution)/shard_map/ppermute | solution.py:320
  32.7 19.1 %collective-permute-start.4 = (bf16[1280,160]{0,1:T(8,128)(2,1)S(1)}, bf16[1280,160]{0,1:T(8,128)(2,1)S(1)}, u32[]{:S(2)}, u32[]{:S(2)}) collective-permute-start(bf16[1280,160]{0,1:T(8,128)(2,1)S(1)} %copy-done.14), channel_id=1, source_target_pairs={{0,2},{1,3},{2,0},{3,1},{4,6},{5,7},{6,4},{7,5},{8,10},{9,11},{10,... | collective-permute-start | bytes 1228808 | tf_op jit(solution)/shard_map/ppermute | solution.py:320
  34.2 18.9 %collective-permute-start = (bf16[16,168,128]{2,1,0:T(8,128)(2,1)S(1)}, bf16[16,168,128]{2,1,0:T(8,128)(2,1)S(1)}, u32[]{:S(2)}, u32[]{:S(2)}) collective-permute-start(bf16[16,168,128]{2,1,0:T(8,128)(2,1)S(1)} %all-to-all-done), channel_id=1, source_target_pairs={{0,4},{4,0},{8,12},{12,8},{16,20},{20,16},{24,28},{28,24},{32,36},... | collective-permute-start | bytes 2064392 | tf_op jit(solution)/shard_map/ppermute | solution.py:332
  53.8 0.8 copy-start.7
  53.8 0.8 copy-start.8
  53.8 0.8 copy-start.10
  54.6 2.2 %copy-start.3 = (bf16[64,128,2,128]{3,2,1,0:T(2,128)(2,1)S(1)}, bf16[64,128,2,128]{3,2,1,0:T(2,128)(2,1)}, u32[]{:S(2)}) copy-start(bf16[64,128,2,128]{3,2,1,0:T(2,128)(2,1)} %param.15) | copy-start | bytes 12582916
  56.8 2.2 %copy-start.5 = (bf16[64,128,2,128]{3,2,1,0:T(2,128)(2,1)S(1)}, bf16[64,128,2,128]{3,2,1,0:T(2,128)(2,1)}, u32[]{:S(2)}) copy-start(bf16[64,128,2,128]{3,2,1,0:T(2,128)(2,1)} %param.16) | copy-start | bytes 12582916
  91.7 21.2 %collective-permute-start.1 = (f32[64,2,30]{2,0,1:T(8,128)S(1)}, f32[64,2,30]{2,0,1:T(8,128)S(1)}, u32[]{:S(2)}, u32[]{:S(2)}) collective-permute-start(f32[64,2,30]{2,0,1:T(8,128)S(1)} %bitcast.124), channel_id=1, source_target_pairs={{0,4},{4,0},{8,12},{12,8},{16,20},{20,16},{24,28},{28,24},{32,36},... | collective-permute-start | bytes 46088 | tf_op jit(solution)/shard_map/ppermute | solution.py:332
  111.1 1.0 copy-start.11
  111.1 1.1 copy-start.12
  111.1 1.2 copy-start.13
  111.8 2.6 %collective-permute-start.2 = (f32[64,30,128]{2,0,1:T(8,128)S(1)}, f32[64,30,128]{2,0,1:T(8,128)S(1)}, u32[]{:S(2)}, u32[]{:S(2)}) collective-permute-start(f32[64,30,128]{2,0,1:T(8,128)S(1)} %bitcast.111), channel_id=1, source_target_pairs={{0,4},{4,0},{8,12},{12,8},{16,20},{20,16},{24,28},{28,24},{32,36},... | collective-permute-start | bytes 2949128 | tf_op jit(solution)/shard_map/ppermute | solution.py:332
  129.2 22.8 %all-to-all-start.2 = ((bf16[64,32,128]{2,1,0:T(8,128)(2,1)}), bf16[64,32,128]{2,1,0:T(8,128)(2,1)S(1)}, u32[]{:S(2)}, u32[]{:S(2)}) async-start(bf16[64,32,128]{2,1,0:T(8,128)(2,1)} %settle.1), calls=%async_computation.2 | async-start | bytes 1048576 | tf_op jit(solution)/shard_map/all_to_all | solution.py:308
  165.0 4.4 %collective-permute-start.6 = (bf16[16,120,128]{2,1,0:T(8,128)(2,1)S(1)}, bf16[16,120,128]{2,1,0:T(8,128)(2,1)S(1)}, u32[]{:S(2)}, u32[]{:S(2)}) collective-permute-start(bf16[16,120,128]{2,1,0:T(8,128)(2,1)S(1)} %all_to_all.20), channel_id=1, source_target_pairs={{0,4},{4,0},{8,12},{12,8},{16,20},{20,16},{24,28},{28,24},{32,36},... | collective-permute-start | bytes 1474568 | tf_op jit(solution)/shard_map/ppermute | solution.py:332
  168.8 2.4 %copy-start.1 = (s32[24,16]{0,1:T(8,128)S(1)}, s32[24,16]{0,1:T(8,128)}, u32[]{:S(2)}) copy-start(s32[24,16]{0,1:T(8,128)} %param.22) | copy-start | bytes 4612

commit v3 on v2

--- a/solution.py
+++ b/solution.py
@@ -10,6 +10,7 @@
 
 CAP = 2
 STEP = 4
+SHIFT = 8
 LOW = -1e30
 
 
@@ -324,8 +325,13 @@
     )
 
 
+def rotate(x, by):
+    return jnp.concatenate([x[by:], x[:by]], axis=0)
+
+
 def in_order(odd, same, other):
-    return jnp.where(odd, jnp.stack([other, same], axis=1), jnp.stack([same, other], axis=1))
+    even_rows, odd_rows = jnp.where(odd, other, same), jnp.where(odd, same, other)
+    return jnp.stack([even_rows, rotate(odd_rows, -SHIFT)], axis=1)
 
 
 def across(x, axis):
@@ -355,7 +361,8 @@
     mine = mine.reshape(-1, head_dim)
     chips = nctx // 2
     odd = (rank & 1) == 1
-    sides = [[2 * i + side for i in range(chips)] for side in range(2)]
+    rings = [[(i + side * SHIFT) % chips for i in range(chips)] for side in range(2)]
+    sides = [[2 * i + side for i in rings[side]] for side in range(2)]
     order = [(d + x) % 4 * 8 + x * 2 + c for d in range(4) for x in range(4) for c in range(2)]
     at = jnp.asarray([order.index(i) for i in range(nctx)], jnp.int32)
     send = pack(me, move_dst, at, keys, values, nctx)
@@ -383,7 +390,8 @@
         lanes = x.shape[-1]
         x = x.reshape(nhead, chips, 2, each, lanes)
         x = jnp.transpose(x, (2, 1, 0, 3, 4)).reshape(2, chips * nhead, each, lanes)
-        return jnp.where(odd, x[1], x[0]), jnp.where(odd, x[0], x[1])
+        even_rows, odd_rows = x[0], rotate(x[1], SHIFT * nhead)
+        return jnp.where(odd, odd_rows, even_rows), jnp.where(odd, even_rows, odd_rows)
 
     kept, given = by_target(numer)
     kept_notes, given_notes = by_target(jnp.swapaxes(stats[:, :2], 1, 2))
@@ -402,7 +410,7 @@
     packet = settle(packet)
     packet, recv, weights = lax.optimization_barrier((packet, recv, weights))
     groups = [
-        [(2 * i + side) * nhead + h for i in range(chips) for h in range(nhead)]
+        [(2 * i + side) * nhead + h for i in rings[side] for h in range(nhead)]
         for side in range(2)
     ]
     parts = exchange(packet, ("ctx", "head"), groups)

time: 172 us -> 170 us (0.988)
  starting transfers between devices: 50.3 us -> 35.4 us
  Pallas kernels: 43.3 us -> 57.8 us
  waiting for transfers between devices: 38.7 us -> 35.9 us
  other arithmetic: 7.21 us -> 5.16 us
  blocking collectives: 11.9 us -> 13.7 us
    ppermute x4, starting transfers between devices: 20.4 us -> 3.5 us  [across(): lax.ppermute(x, axis, [(i, i ^ 1) for i in range(lax.axis_size(axis))])]
    pallas_call x1, Pallas kernels: 32.3 us -> 47.2 us  [attention(): pl.pallas_call(functools.partial(attention_kernel, kv_local, group, log_s...]
    all_to_all x3, waiting for transfers between devices: 20.8 us -> 17.6 us  [exchange(): lax.all_to_all(x, axis, split_axis=0, concat_axis=0, tiled=True, axis_ind...]
    all_to_all x3, starting transfers between devices: 25.4 us -> 27.4 us  [exchange(): lax.all_to_all(x, axis, split_axis=0, concat_axis=0, tiled=True, axis_ind...]
    select_n x4 -> x1, other arithmetic: 2.21 us -> 0.23 us  [by_target(): jnp.where(odd, even_rows, odd_rows)]
    slice x0 -> x14, local copies, waits for them, and re-layouts: none -> 1.91 us  [the longest x4 1.6 us: by_target(): even_rows, odd_rows = (x[0], rotate(x[1], SHIFT * nhead))]
    all_to_all x1, blocking collectives: 11.9 us -> 13.7 us  [exchange(): lax.all_to_all(x, axis, split_axis=0, concat_axis=0, tiled=True, axis_ind...]
    unnamed x31 -> x33, local copies, waits for them, and re-layouts: 10 us -> 9.96 us
  transfers between devices with their start and end apart: 10 -> 10, of which waited for: 7 -> 7; matrix products, arithmetic and copies ran while one was open for 7% -> 7% of each run, Pallas kernels for 25% -> 34%
where the time goes in v3:
time: 170 us; the launch traced here: 169 us
  Pallas kernels  57.8 us (34%)
  waiting for transfers between devices  35.9 us (21%)
  starting transfers between devices  35.4 us (21%)
  local copies, waits for them, and re-layouts  19.1 us (11%)
  blocking collectives  13.7 us (8%)
  other arithmetic  5.16 us (3%)
    pallas_call x1, Pallas kernels, attention(): pl.pallas_call(functools.partial(attention_kernel, kv_local, group, log_s...  47.2 us
    all_to_all x3, starting transfers between devices, exchange(): lax.all_to_all(x, axis, split_axis=0, concat_axis=0, tiled=True, axis_ind...  27.4 us
    all_to_all x3, waiting for transfers between devices, exchange(): lax.all_to_all(x, axis, split_axis=0, concat_axis=0, tiled=True, axis_ind...  17.6 us
    ppermute x3, waiting for transfers between devices, around(): lax.ppermute(x, axis, [(i, (i + d) % n) for i in range(n)])  16.2 us
    all_to_all x1, blocking collectives, exchange(): lax.all_to_all(x, axis, split_axis=0, concat_axis=0, tiled=True, axis_ind...  13.7 us
    unnamed x33, local copies, waits for them, and re-layouts  9.96 us
    pallas_call x1, Pallas kernels, unpack(): pl.pallas_call(functools.partial(unpack_kernel, slots), out_shape=(shape,...  4.46 us
    ppermute x3, starting transfers between devices, around(): lax.ppermute(x, axis, [(i, (i + d) % n) for i in range(n)])  4.45 us
  transfers between devices with their start and end apart: 10, of which 7 were waited for; matrix products, arithmetic and copies ran while one was open for 7% of the time, Pallas kernels for 34%

profile of v3, /device:TPU:1, one launch (start us, length us, event | category | flops | bytes accessed | tf_op | source)
XLA Modules:
  0.0 169.5 jit_solution(11291170552270829109)
XLA Ops:
  0.7 0.8 pad_maximum_fusion.5
  1.6 0.9 broadcast_in_dim.26
  2.5 9.5 %all-to-all-start = ((bf16[16,168,128]{2,1,0:T(8,128)(2,1)}), bf16[16,168,128]{2,1,0:T(8,128)(2,1)S(1)}, u32[]{:S(2)}, u32[]{:S(2)}) async-start(bf16[16,168,128]{2,1,0:T(8,128)(2,1)} %broadcast_in_dim.26), calls=%async_computation | async-start | bytes 1376256 | tf_op jit(solution)/shard_map/all_to_all | solution.py:309
  12.1 2.2 %copy-done.2 = bf16[64,128,2,128]{3,2,1,0:T(2,128)(2,1)S(1)} copy-done((bf16[64,128,2,128]{3,2,1,0:T(2,128)(2,1)S(1)}, bf16[64,128,2,128]{3,2,1,0:T(2,128)(2,1)}, u32[]{:S(2)}) %copy-start.2) | copy-done | bytes 4194328
  14.3 2.2 %copy-done.4 = bf16[64,128,2,128]{3,2,1,0:T(2,128)(2,1)S(1)} copy-done((bf16[64,128,2,128]{3,2,1,0:T(2,128)(2,1)S(1)}, bf16[64,128,2,128]{3,2,1,0:T(2,128)(2,1)}, u32[]{:S(2)}) %copy-start.4) | copy-done | bytes 4194328
  16.4 4.2 %pack.1 = bf16[128,256,128]{2,1,0:T(8,128)(2,1)} custom-call(s32[1]{0:T(128)} %bitcast.rank_ref, s32[2048]{0:T(1024)S(1)} %copy-done.6, s32[32]{0:T(128)S(1)} %copy-done.9, bf16[64,256,128]{2,1,0:T(8,128)(2,1)S(1)} %bitcast.107, bf16[64,256,128]{2,1,0:T(8,128)(2,1)S(1)} %bitcast.109), custom_call_target="tpu_custom_call" | custom-call | bytes 16777216 | tf_op jit(solution)/shard_map/pack/pallas_call | solution.py:60
  20.7 1.3 all-to-all-done
  22.0 6.8 %all-to-all-start.1 = ((bf16[128,256,128]{2,1,0:T(8,128)(2,1)}), bf16[128,256,128]{2,1,0:T(8,128)(2,1)}, u32[]{:S(2)}, u32[]{:S(2)}) async-start(bf16[128,256,128]{2,1,0:T(8,128)(2,1)} %pack.1), calls=%async_computation.1 | async-start | bytes 16777216 | tf_op jit(solution)/shard_map/all_to_all | solution.py:309
  28.8 1.4 collective-permute-start.3
  30.2 1.5 collective-permute-start.5
  31.7 1.6 collective-permute-start.4
  33.3 1.1 collective-permute-start
  34.8 6.3 %collective-permute-done.3 = bf16[1280,160]{0,1:T(8,128)(2,1)S(1)} collective-permute-done((bf16[1280,160]{0,1:T(8,128)(2,1)S(1)}, bf16[1280,160]{0,1:T(8,128)(2,1)S(1)}, u32[]{:S(2)}, u32[]{:S(2)}) %collective-permute-start.3) | collective-permute-done | bytes 409632 | tf_op jit(solution)/shard_map/ppermute | solution.py:321
  41.1 9.9 %collective-permute-done.4 = bf16[1280,160]{0,1:T(8,128)(2,1)S(1)} collective-permute-done((bf16[1280,160]{0,1:T(8,128)(2,1)S(1)}, bf16[1280,160]{0,1:T(8,128)(2,1)S(1)}, u32[]{:S(2)}, u32[]{:S(2)}) %collective-permute-start.4) | collective-permute-done | bytes 409632 | tf_op jit(solution)/shard_map/ppermute | solution.py:321
  51.0 0.2 pad_maximum_fusion
  51.2 1.1 constant_dynamic-slice_fusion.3
  52.6 0.4 reshape.146
  53.1 0.4 reshape.147.q_ref
  53.5 0.4 fusion.12
  53.9 2.2 %copy-done.3 = bf16[64,128,2,128]{3,2,1,0:T(2,128)(2,1)S(1)} copy-done((bf16[64,128,2,128]{3,2,1,0:T(2,128)(2,1)S(1)}, bf16[64,128,2,128]{3,2,1,0:T(2,128)(2,1)}, u32[]{:S(2)}) %copy-start.3) | copy-done | bytes 4194328
  56.1 2.2 %copy-done.5 = bf16[64,128,2,128]{3,2,1,0:T(2,128)(2,1)S(1)} copy-done((bf16[64,128,2,128]{3,2,1,0:T(2,128)(2,1)S(1)}, bf16[64,128,2,128]{3,2,1,0:T(2,128)(2,1)}, u32[]{:S(2)}) %copy-start.5) | copy-done | bytes 4194328
  58.3 47.2 %attention.1 = (f32[24,160,128]{2,1,0:T(8,128)S(1)}, f32[24,8,160]{2,1,0:T(8,128)S(1)}, bf16[96,256,128]{2,1,0:T(8,128)(2,1)}, bf16[96,256,128]{2,1,0:T(8,128)(2,1)}) custom-call(s32[1]{0:T(128)} %bitcast.rank_ref, s32[2048]{0:T(1024)S(1)} %copy-done.7, s32[2048]{0:T(1024)S(1)} %copy-done.8, s32[2048]{0:T(1024)S(1)} %copy-done.6, s32[24]{0:T(128)S(1)} %copy-done.10, ...), custom_call_target="tpu_custom_call" | custom-call | flops 1342177280 | bytes 16777216 | tf_op jit(solution)/shard_map/attention/pallas_call | solution.py:268
  105.5 0.3 reshape.151
  106.1 1.5 reshape.150
  107.5 1.5 slice.136
  109.1 0.4 copy-done.11
  109.6 0.2 bitcast_select_fusion
  109.9 0.6 copy.88
  110.5 0.6 collective-permute-start.2
  111.1 0.2 maximum_bitcast_fusion
  111.7 1.5 collective-permute-done.2
  113.2 1.0 fusion.2
  114.3 1.0 fusion.4.x_ref
  115.2 1.9 %settle.1 = bf16[64,32,128]{2,1,0:T(8,128)(2,1)} custom-call(bf16[64,32,128]{2,1,0:T(8,128)(2,1)} %fusion.4.x_ref), custom_call_target="tpu_custom_call" | custom-call | tf_op jit(solution)/shard_map/settle/pallas_call | solution.py:303
  117.1 11.0 %all-to-all-done.1.recv_ref = bf16[128,256,128]{2,1,0:T(8,128)(2,1)} async-done(((bf16[128,256,128]{2,1,0:T(8,128)(2,1)}), bf16[128,256,128]{2,1,0:T(8,128)(2,1)}, u32[]{:S(2)}, u32[]{:S(2)}) %all-to-all-start.1) | async-done | bytes 8388640 | tf_op jit(solution)/shard_map/all_to_all | solution.py:309
  128.1 11.1 %all-to-all-start.2 = ((bf16[64,32,128]{2,1,0:T(8,128)(2,1)}), bf16[64,32,128]{2,1,0:T(8,128)(2,1)S(1)}, u32[]{:S(2)}, u32[]{:S(2)}) async-start(bf16[64,32,128]{2,1,0:T(8,128)(2,1)} %settle.1), calls=%async_computation.2 | async-start | bytes 1048576 | tf_op jit(solution)/shard_map/all_to_all | solution.py:309
  139.3 0.6 reduce_sum.29.count_ref
  139.9 4.5 %unpack.1 = (bf16[96,256,128]{2,1,0:T(8,128)(2,1)}, bf16[96,256,128]{2,1,0:T(8,128)(2,1)}) custom-call(s32[32]{0:T(128)} %reduce_sum.29.count_ref, s32[32]{0:T(128)} %constant.53.clone.at_ref, bf16[128,256,128]{2,1,0:T(8,128)(2,1)} %all-to-all-done.1.recv_ref, ...), custom_call_target="tpu_custom_call", output_to_operand_aliasing={{0}: (3, {}), {1}: (4, {})} | custom-call | bytes 8388608 | tf_op jit(solution)/shard_map/unpack/pallas_call | solution.py:134
  144.4 5.3 %all-to-all-done.2 = bf16[64,32,128]{2,1,0:T(8,128)(2,1)S(1)} async-done(((bf16[64,32,128]{2,1,0:T(8,128)(2,1)}), bf16[64,32,128]{2,1,0:T(8,128)(2,1)S(1)}, u32[]{:S(2)}, u32[]{:S(2)}) %all-to-all-start.2) | async-done | bytes 524320 | tf_op jit(solution)/shard_map/all_to_all | solution.py:309
  150.2 0.3 multiply_reduce_fusion
  150.8 13.7 %all_to_all.20 = bf16[16,120,128]{2,1,0:T(8,128)(2,1)S(1)} all-to-all(bf16[16,120,128]{2,1,0:T(8,128)(2,1)S(1)} %broadcast_in_dim.30), channel_id=1, replica_groups={{0,8,16,24,32,40,48,56,64,72,80,88,96,104,112,120},{68,76,84,92,100,108..., dimensions={0} | all-to-all | bytes 983040 | tf_op jit(solution)/shard_map/all_to_all | solution.py:309
  164.5 1.7 collective-permute-start.6
  166.1 0.2 reshape.155
  166.4 0.6 convolution_convert_fusion
  167.0 0.6 collective-permute-done.6
  167.6 0.2 reshape.154
  167.8 0.6 broadcast_select_fusion.2
  168.8 0.7 copy.99
  (81 shorter events, 2.7 us)
Async XLA Ops:
  0.6 33.8 %copy-start = (s32[24,16]{0,1:T(8,128)S(1)}, s32[24,16]{0,1:T(8,128)}, u32[]{:S(2)}) copy-start(s32[24,16]{0,1:T(8,128)} %param.22) | copy-start | bytes 4612
  0.6 11.4 %copy-start.9 = (s32[32]{0:T(128)S(1)}, s32[32]{0:T(128)}, u32[]{:S(2)}) copy-start(s32[32]{0:T(128)} %constant.53.clone.at_ref) | copy-start | bytes 388
  0.7 11.4 %copy-start.6 = (s32[2048]{0:T(1024)S(1)}, s32[2048]{0:T(1024)}, u32[]{:S(2)}) copy-start(s32[2048]{0:T(1024)} %dst_ref.3) | copy-start | bytes 24580
  2.5 19.5 %all-to-all-start = ((bf16[16,168,128]{2,1,0:T(8,128)(2,1)}), bf16[16,168,128]{2,1,0:T(8,128)(2,1)S(1)}, u32[]{:S(2)}, u32[]{:S(2)}) async-start(bf16[16,168,128]{2,1,0:T(8,128)(2,1)} %broadcast_in_dim.26), calls=%async_computation | async-start | bytes 1376256 | tf_op jit(solution)/shard_map/all_to_all | solution.py:309
  12.1 2.2 %copy-start.2 = (bf16[64,128,2,128]{3,2,1,0:T(2,128)(2,1)S(1)}, bf16[64,128,2,128]{3,2,1,0:T(2,128)(2,1)}, u32[]{:S(2)}) copy-start(bf16[64,128,2,128]{3,2,1,0:T(2,128)(2,1)} %param.15) | copy-start | bytes 12582916
  14.3 2.2 %copy-start.4 = (bf16[64,128,2,128]{3,2,1,0:T(2,128)(2,1)S(1)}, bf16[64,128,2,128]{3,2,1,0:T(2,128)(2,1)}, u32[]{:S(2)}) copy-start(bf16[64,128,2,128]{3,2,1,0:T(2,128)(2,1)} %param.16) | copy-start | bytes 12582916
  20.7 8.2 %copy-start.15 = (bf16[1280,160]{0,1:T(8,128)(2,1)S(1)}, bf16[1280,160]{0,1:T(8,128)(2,1)}, u32[]{:S(2)}) copy-start(bf16[1280,160]{0,1:T(8,128)(2,1)} %param.17) | copy-start | bytes 1228804
  22.0 106.0 %all-to-all-start.1 = ((bf16[128,256,128]{2,1,0:T(8,128)(2,1)}), bf16[128,256,128]{2,1,0:T(8,128)(2,1)}, u32[]{:S(2)}, u32[]{:S(2)}) async-start(bf16[128,256,128]{2,1,0:T(8,128)(2,1)} %pack.1), calls=%async_computation.1 | async-start | bytes 16777216 | tf_op jit(solution)/shard_map/all_to_all | solution.py:309
  28.8 12.3 %collective-permute-start.3 = (bf16[1280,160]{0,1:T(8,128)(2,1)S(1)}, bf16[1280,160]{0,1:T(8,128)(2,1)S(1)}, u32[]{:S(2)}, u32[]{:S(2)}) collective-permute-start(bf16[1280,160]{0,1:T(8,128)(2,1)S(1)} %copy-done.15), channel_id=1, source_target_pairs={{0,1},{1,2},{2,3},{3,0},{4,5},{5,6},{6,7},{7,4},{8,9},{9,10},{10,1... | collective-permute-start | bytes 1228808 | tf_op jit(solution)/shard_map/ppermute | solution.py:321
  30.2 10.9 %collective-permute-start.5 = (bf16[1280,160]{0,1:T(8,128)(2,1)S(1)}, bf16[1280,160]{0,1:T(8,128)(2,1)S(1)}, u32[]{:S(2)}, u32[]{:S(2)}) collective-permute-start(bf16[1280,160]{0,1:T(8,128)(2,1)S(1)} %copy-done.15), channel_id=1, source_target_pairs={{0,3},{1,0},{2,1},{3,2},{4,7},{5,4},{6,5},{7,6},{8,11},{9,8},{10,9... | collective-permute-start | bytes 1228808 | tf_op jit(solution)/shard_map/ppermute | solution.py:321
  31.7 19.3 %collective-permute-start.4 = (bf16[1280,160]{0,1:T(8,128)(2,1)S(1)}, bf16[1280,160]{0,1:T(8,128)(2,1)S(1)}, u32[]{:S(2)}, u32[]{:S(2)}) collective-permute-start(bf16[1280,160]{0,1:T(8,128)(2,1)S(1)} %copy-done.15), channel_id=1, source_target_pairs={{0,2},{1,3},{2,0},{3,1},{4,6},{5,7},{6,4},{7,5},{8,10},{9,11},{10,... | collective-permute-start | bytes 1228808 | tf_op jit(solution)/shard_map/ppermute | solution.py:321
  33.3 19.0 %collective-permute-start = (bf16[16,168,128]{2,1,0:T(8,128)(2,1)S(1)}, bf16[16,168,128]{2,1,0:T(8,128)(2,1)S(1)}, u32[]{:S(2)}, u32[]{:S(2)}) collective-permute-start(bf16[16,168,128]{2,1,0:T(8,128)(2,1)S(1)} %all-to-all-done), channel_id=1, source_target_pairs={{0,4},{4,0},{8,12},{12,8},{16,20},{20,16},{24,28},{28,24},{32,36},... | collective-permute-start | bytes 2064392 | tf_op jit(solution)/shard_map/ppermute | solution.py:338
  53.1 0.8 copy-start.7
  53.1 0.8 copy-start.8
  53.1 0.8 copy-start.10
  53.9 2.2 %copy-start.3 = (bf16[64,128,2,128]{3,2,1,0:T(2,128)(2,1)S(1)}, bf16[64,128,2,128]{3,2,1,0:T(2,128)(2,1)}, u32[]{:S(2)}) copy-start(bf16[64,128,2,128]{3,2,1,0:T(2,128)(2,1)} %param.15) | copy-start | bytes 12582916
  56.1 2.2 %copy-start.5 = (bf16[64,128,2,128]{3,2,1,0:T(2,128)(2,1)S(1)}, bf16[64,128,2,128]{3,2,1,0:T(2,128)(2,1)}, u32[]{:S(2)}) copy-start(bf16[64,128,2,128]{3,2,1,0:T(2,128)(2,1)} %param.16) | copy-start | bytes 12582916
  106.0 5.5 %collective-permute-start.1 = (f32[64,2,30]{2,0,1:T(8,128)S(1)}, f32[64,2,30]{2,0,1:T(8,128)S(1)}, u32[]{:S(2)}, u32[]{:S(2)}) collective-permute-start(f32[64,2,30]{2,0,1:T(8,128)S(1)} %get-tuple-element.65), channel_id=1, source_target_pairs={{0,4},{4,0},{8,12},{12,8},{16,20},{20,16},{24,28},{28,24},{32,36},... | collective-permute-start | bytes 46088 | tf_op jit(solution)/shard_map/ppermute | solution.py:338
  107.5 1.9 %copy-start.11 = (f32[4,16,2,30,128]{4,3,2,1,0:T(8,128)S(1)}, f32[4,16,2,30,128]{4,3,2,1,0:T(8,128)}, u32[]{:S(2)}) copy-start(f32[4,16,2,30,128]{4,3,2,1,0:T(8,128)} %reshape.150) | copy-start | bytes 5898244
  109.9 1.2 copy-start.12
  109.9 1.2 copy-start.13
  109.9 1.2 copy-start.14
  110.5 2.8 %collective-permute-start.2 = (f32[64,30,128]{2,0,1:T(8,128)S(1)}, f32[64,30,128]{2,0,1:T(8,128)S(1)}, u32[]{:S(2)}, u32[]{:S(2)}) collective-permute-start(f32[64,30,128]{2,0,1:T(8,128)S(1)} %copy.88), channel_id=1, source_target_pairs={{0,4},{4,0},{8,12},{12,8},{16,20},{20,16},{24,28},{28,24},{32,36},... | collective-permute-start | bytes 2949128 | tf_op jit(solution)/shard_map/ppermute | solution.py:338
  128.1 21.6 %all-to-all-start.2 = ((bf16[64,32,128]{2,1,0:T(8,128)(2,1)}), bf16[64,32,128]{2,1,0:T(8,128)(2,1)S(1)}, u32[]{:S(2)}, u32[]{:S(2)}) async-start(bf16[64,32,128]{2,1,0:T(8,128)(2,1)} %settle.1), calls=%async_computation.2 | async-start | bytes 1048576 | tf_op jit(solution)/shard_map/all_to_all | solution.py:309
  164.5 3.2 %collective-permute-start.6 = (bf16[16,120,128]{2,1,0:T(8,128)(2,1)S(1)}, bf16[16,120,128]{2,1,0:T(8,128)(2,1)S(1)}, u32[]{:S(2)}, u32[]{:S(2)}) collective-permute-start(bf16[16,120,128]{2,1,0:T(8,128)(2,1)S(1)} %all_to_all.20), channel_id=1, source_target_pairs={{0,4},{4,0},{8,12},{12,8},{16,20},{20,16},{24,28},{28,24},{32,36},... | collective-permute-start | bytes 1474568 | tf_op jit(solution)/shard_map/ppermute | solution.py:338
  167.6 1.8 %copy-start.1 = (s32[24,16]{0,1:T(8,128)S(1)}, s32[24,16]{0,1:T(8,128)}, u32[]{:S(2)}) copy-start(s32[24,16]{0,1:T(8,128)} %param.22) | copy-start | bytes 4612

commit v4 on v3

--- a/solution.py
+++ b/solution.py
@@ -70,7 +70,7 @@
                 pltpu.SemaphoreType.DMA((blocks, 2)),
             ],
         ),
-        compiler_params=pltpu.CompilerParams(vmem_limit_bytes=40 * 2**20),
+        compiler_params=pltpu.CompilerParams(vmem_limit_bytes=58 * 2**20),
         cost_estimate=pl.CostEstimate(
             flops=0, bytes_accessed=4 * blocks * rows * lanes * 2, transcendentals=0
         ),
@@ -207,14 +207,15 @@
         own = row % (kv_local * group) // group
         column[...] = jnp.where(line % kv_local == own, line // kv_local, 1 << 20)
 
-        @pl.when(rank < requests)
-        def _():
-            drafts = dk_ref.shape[1]
+        @pl.when((rank & 3) < 3)
+        def _():
+            drafts = dk_ref.shape[0]
+            mine = 3 * (rank >> 2) + (rank & 3)
             spot = column[:, :drafts]
             spot = jnp.where(spot >= offs_ref[...], spot, 1 << 20)
             token = lax.broadcasted_iota(jnp.int32, spot.shape, 0) // (kv_local * group)
-            attend(q_ref[rank], dk_ref[rank], dv_ref[rank], spot, token + 1,
-                   top, total, numer, rank, log_scale)
+            attend(q_ref[mine], dk_ref[...], dv_ref[...], spot, token + 1,
+                   top, total, numer, mine, log_scale)
 
     for g in range(STEP):
         slot = base + g
@@ -357,8 +358,9 @@
     keys = cache_keys.reshape(blocks, width * kv_local, head_dim)
     values = cache_values.reshape(blocks, width * kv_local, head_dim)
 
-    mine = jnp.concatenate([queries, draft_keys, draft_values], axis=1)
-    mine = mine.reshape(-1, head_dim)
+    mine = queries.reshape(-1, head_dim)
+    pair = jnp.concatenate([draft_keys, draft_values], axis=1)
+    after = lax.ppermute(pair, "ctx", [(i, (i - 1) % nctx) for i in range(nctx)])
     chips = nctx // 2
     odd = (rank & 1) == 1
     rings = [[(i + side * SHIFT) % chips for i in range(chips)] for side in range(2)]
@@ -367,18 +369,22 @@
     at = jnp.asarray([order.index(i) for i in range(nctx)], jnp.int32)
     send = pack(me, move_dst, at, keys, values, nctx)
     same = everywhere(mine, "ctx", sides)
-    same, send = lax.optimization_barrier((same, send))
+    same, send, after = lax.optimization_barrier((same, send, after))
     recv = exchange(send, "ctx", [order])
     other = across(same, "ctx")
     shared = in_order(odd, same, other)
-    shared = shared.reshape(tokens, heads + 2 * kv_local, head_dim)
-    q = shared[:, :heads].reshape(requests, drafts * heads, head_dim)
-    dk = shared[:, heads : heads + kv_local].reshape(requests, drafts * kv_local, head_dim)
-    dv = shared[:, heads + kv_local :].reshape(requests, drafts * kv_local, head_dim)
+    q = shared.reshape(requests, drafts * heads, head_dim)
+    span = jnp.concatenate([pair, after], axis=0)
+    span = lax.dynamic_slice_in_dim(span, (rank & 3) * (drafts - own), drafts)
+    dk, dv = (
+        x.reshape(drafts * kv_local, head_dim)
+        for x in (span[:, : kv_local * head_dim], span[:, kv_local * head_dim :])
+    )
     nhead = lax.axis_size("head")
     weights = around(w_out, "head").reshape(nhead * heads * head_dim, -1)
 
-    my_offs = lax.dynamic_slice_in_dim(draft_offs, jnp.minimum(rank, requests - 1), 1)[0]
+    my_req = jnp.minimum(3 * (rank >> 2) + (rank & 3), requests - 1)
+    my_offs = lax.dynamic_slice_in_dim(draft_offs, my_req, 1)[0]
     offs = jnp.repeat(my_offs, heads)[:, None]
     numer, stats, new_keys, new_values = attention(
         me, block_req, block_idx, move_dst, lengths, q, dk, dv, offs, keys, values,

time: 170 us -> 169 us (level)
  starting transfers between devices: 35.4 us -> 52.2 us
  Pallas kernels: 57.8 us -> 44.1 us
  local copies, waits for them, and re-layouts: 19.1 us -> 15.4 us
    pallas_call x1, Pallas kernels: 47.2 us -> 31.3 us  [attention(): pl.pallas_call(functools.partial(attention_kernel, kv_local, group, log_s...]
    ppermute x4, starting transfers between devices: 3.5 us -> 19.3 us  [across(): lax.ppermute(x, axis, [(i, i ^ 1) for i in range(lax.axis_size(axis))])]
    unnamed x33 -> x24, local copies, waits for them, and re-layouts: 9.96 us -> 6.21 us
    all_to_all x3, waiting for transfers between devices: 17.6 us -> 15 us  [exchange(): lax.all_to_all(x, axis, split_axis=0, concat_axis=0, tiled=True, axis_ind...]
  transfers between devices with their start and end apart: 10 -> 11, of which waited for: 7 -> 8; matrix products, arithmetic and copies ran while one was open for 7% -> 7% of each run, Pallas kernels for 34% -> 26%
where the time goes in v4:
time: 169 us; the launch traced here: 168 us
  starting transfers between devices  52.2 us (31%)
  Pallas kernels  44.1 us (26%)
  waiting for transfers between devices  36.4 us (22%)
  local copies, waits for them, and re-layouts  15.4 us (9%)
  blocking collectives  13.7 us (8%)
  other arithmetic  4.26 us (3%)
    pallas_call x1, Pallas kernels, attention(): pl.pallas_call(functools.partial(attention_kernel, kv_local, group, log_s...  31.3 us
    all_to_all x3, starting transfers between devices, exchange(): lax.all_to_all(x, axis, split_axis=0, concat_axis=0, tiled=True, axis_ind...  28.5 us
    ppermute x4, starting transfers between devices, across(): lax.ppermute(x, axis, [(i, i ^ 1) for i in range(lax.axis_size(axis))])  19.3 us
    ppermute x3, waiting for transfers between devices, around(): lax.ppermute(x, axis, [(i, (i + d) % n) for i in range(n)])  17.3 us
    all_to_all x3, waiting for transfers between devices, exchange(): lax.all_to_all(x, axis, split_axis=0, concat_axis=0, tiled=True, axis_ind...  15 us
    all_to_all x1, blocking collectives, exchange(): lax.all_to_all(x, axis, split_axis=0, concat_axis=0, tiled=True, axis_ind...  13.7 us
    unnamed x24, local copies, waits for them, and re-layouts  6.21 us
    pallas_call x1, Pallas kernels, unpack(): pl.pallas_call(functools.partial(unpack_kernel, slots), out_shape=(shape,...  5.55 us
  transfers between devices with their start and end apart: 11, of which 8 were waited for; matrix products, arithmetic and copies ran while one was open for 7% of the time, Pallas kernels for 26%

profile of v4, /device:TPU:1, one launch (start us, length us, event | category | flops | bytes accessed | tf_op | source)
XLA Modules:
  0.0 168.5 jit_solution(11622690498970394476)
XLA Ops:
  0.6 0.9 broadcast_in_dim.12
  1.5 0.8 broadcast_in_dim.26
  2.3 9.5 %all-to-all-start = ((bf16[16,120,128]{2,1,0:T(8,128)(2,1)}), bf16[16,120,128]{2,1,0:T(8,128)(2,1)S(1)}, u32[]{:S(2)}, u32[]{:S(2)}) async-start(bf16[16,120,128]{2,1,0:T(8,128)(2,1)} %broadcast_in_dim.26), calls=%async_computation | async-start | bytes 983040 | tf_op jit(solution)/shard_map/all_to_all | solution.py:310
  11.9 0.7 constant_dynamic-update-slice_fusion.1
  12.6 0.7 constant_dynamic-update-slice_fusion
  13.3 5.4 %pack.1 = bf16[128,256,128]{2,1,0:T(8,128)(2,1)} custom-call(s32[1]{0:T(128)} %bitcast.rank_ref, s32[2048]{0:T(1024)} %dst_ref.3, s32[32]{0:T(128)} %constant.55.clone.at_ref, bf16[64,256,128]{2,1,0:T(8,128)(2,1)} %bitcast.103, bf16[64,256,128]{2,1,0:T(8,128)(2,1)} %bitcast.105), custom_call_target="tpu_custom_call" | custom-call | bytes 16777216 | tf_op jit(solution)/shard_map/pack/pallas_call | solution.py:60
  18.7 1.3 collective-permute-done
  20.0 7.8 %all-to-all-start.1 = ((bf16[128,256,128]{2,1,0:T(8,128)(2,1)}), bf16[128,256,128]{2,1,0:T(8,128)(2,1)}, u32[]{:S(2)}, u32[]{:S(2)}) async-start(bf16[128,256,128]{2,1,0:T(8,128)(2,1)} %pack.1), calls=%async_computation.1 | async-start | bytes 16777216 | tf_op jit(solution)/shard_map/all_to_all | solution.py:310
  27.9 1.4 collective-permute-start.4
  29.2 1.5 collective-permute-start.6
  30.7 1.6 collective-permute-start.5
  32.3 0.2 dynamic-slice_reduce_fusion
  32.7 7.5 %collective-permute-done.4 = bf16[1280,160]{0,1:T(8,128)(2,1)S(1)} collective-permute-done((bf16[1280,160]{0,1:T(8,128)(2,1)S(1)}, bf16[1280,160]{0,1:T(8,128)(2,1)S(1)}, u32[]{:S(2)}, u32[]{:S(2)}) %collective-permute-start.4) | collective-permute-done | bytes 409632 | tf_op jit(solution)/shard_map/ppermute | solution.py:322
  40.1 9.9 %collective-permute-done.5 = bf16[1280,160]{0,1:T(8,128)(2,1)S(1)} collective-permute-done((bf16[1280,160]{0,1:T(8,128)(2,1)S(1)}, bf16[1280,160]{0,1:T(8,128)(2,1)S(1)}, u32[]{:S(2)}, u32[]{:S(2)}) %collective-permute-start.5) | collective-permute-done | bytes 409632 | tf_op jit(solution)/shard_map/ppermute | solution.py:322
  50.0 0.2 pad_maximum_fusion
  50.2 1.1 collective-permute-start.1
  51.3 0.9 constant_dynamic-slice_fusion.3
  52.3 0.5 collective-permute-done.1
  53.1 1.9 %copy-done.2 = bf16[64,128,2,128]{3,2,1,0:T(2,128)(2,1)S(1)} copy-done((bf16[64,128,2,128]{3,2,1,0:T(2,128)(2,1)S(1)}, bf16[64,128,2,128]{3,2,1,0:T(2,128)(2,1)}, u32[]{:S(2)}) %copy-start.2) | copy-done | bytes 4194328
  55.0 2.2 %copy-done.3 = bf16[64,128,2,128]{3,2,1,0:T(2,128)(2,1)S(1)} copy-done((bf16[64,128,2,128]{3,2,1,0:T(2,128)(2,1)S(1)}, bf16[64,128,2,128]{3,2,1,0:T(2,128)(2,1)}, u32[]{:S(2)}) %copy-start.3) | copy-done | bytes 4194328
  57.2 31.3 %attention.1 = (f32[24,160,128]{2,1,0:T(8,128)S(1)}, f32[24,8,160]{2,1,0:T(8,128)S(1)}, bf16[96,256,128]{2,1,0:T(8,128)(2,1)}, bf16[96,256,128]{2,1,0:T(8,128)(2,1)}) custom-call(s32[1]{0:T(128)} %bitcast.rank_ref, s32[2048]{0:T(1024)S(1)} %copy-done.5, s32[2048]{0:T(1024)S(1)} %copy-done.6, s32[2048]{0:T(1024)S(1)} %copy-done.4, s32[24]{0:T(128)S(1)} %copy-done.7, ...), custom_call_target="tpu_custom_call" | custom-call | flops 1342177280 | bytes 16777216 | tf_op jit(solution)/shard_map/attention/pallas_call | solution.py:269
  88.5 0.3 reshape.147
  89.0 16.4 %collective-permute-start.2 = (f32[64,2,30]{2,0,1:T(8,128)S(1)}, f32[64,2,30]{2,0,1:T(8,128)S(1)}, u32[]{:S(2)}, u32[]{:S(2)}) collective-permute-start(f32[64,2,30]{2,0,1:T(8,128)S(1)} %get-tuple-element.65), channel_id=1, source_target_pairs={{0,4},{4,0},{8,12},{12,8},{16,20},{20,16},{24,28},{28,24},{32,36},... | collective-permute-start | bytes 46088 | tf_op jit(solution)/shard_map/ppermute | solution.py:339
  105.4 1.5 reshape.146
  106.9 1.5 slice.131
  108.5 0.4 copy-done.8
  109.0 0.2 bitcast_select_fusion
  109.3 0.6 copy.88
  109.9 0.3 copy-done.9
  110.3 0.2 maximum_bitcast_fusion
  110.8 1.6 collective-permute-done.3
  112.5 1.0 fusion.2
  113.5 0.9 fusion.4.x_ref
  114.5 1.9 %settle.1 = bf16[64,32,128]{2,1,0:T(8,128)(2,1)} custom-call(bf16[64,32,128]{2,1,0:T(8,128)(2,1)} %fusion.4.x_ref), custom_call_target="tpu_custom_call" | custom-call | tf_op jit(solution)/shard_map/settle/pallas_call | solution.py:304
  116.3 10.8 %all-to-all-done.1.recv_ref = bf16[128,256,128]{2,1,0:T(8,128)(2,1)} async-done(((bf16[128,256,128]{2,1,0:T(8,128)(2,1)}), bf16[128,256,128]{2,1,0:T(8,128)(2,1)}, u32[]{:S(2)}, u32[]{:S(2)}) %all-to-all-start.1) | async-done | bytes 8388640 | tf_op jit(solution)/shard_map/all_to_all | solution.py:310
  127.1 11.1 %all-to-all-start.2 = ((bf16[64,32,128]{2,1,0:T(8,128)(2,1)}), bf16[64,32,128]{2,1,0:T(8,128)(2,1)S(1)}, u32[]{:S(2)}, u32[]{:S(2)}) async-start(bf16[64,32,128]{2,1,0:T(8,128)(2,1)} %settle.1), calls=%async_computation.2 | async-start | bytes 1048576 | tf_op jit(solution)/shard_map/all_to_all | solution.py:310
  138.3 0.6 reduce_sum.29.count_ref
  138.9 5.5 %unpack.1 = (bf16[96,256,128]{2,1,0:T(8,128)(2,1)}, bf16[96,256,128]{2,1,0:T(8,128)(2,1)}) custom-call(s32[32]{0:T(128)} %reduce_sum.29.count_ref, s32[32]{0:T(128)} %constant.55.clone.at_ref, bf16[128,256,128]{2,1,0:T(8,128)(2,1)} %all-to-all-done.1.recv_ref, ...), custom_call_target="tpu_custom_call", output_to_operand_aliasing={{0}: (3, {}), {1}: (4, {})} | custom-call | bytes 8388608 | tf_op jit(solution)/shard_map/unpack/pallas_call | solution.py:134
  144.5 4.2 %all-to-all-done.2 = bf16[64,32,128]{2,1,0:T(8,128)(2,1)S(1)} async-done(((bf16[64,32,128]{2,1,0:T(8,128)(2,1)}), bf16[64,32,128]{2,1,0:T(8,128)(2,1)S(1)}, u32[]{:S(2)}, u32[]{:S(2)}) %all-to-all-start.2) | async-done | bytes 524320 | tf_op jit(solution)/shard_map/all_to_all | solution.py:310
  149.2 0.3 multiply_reduce_fusion
  149.8 13.7 %all_to_all.20 = bf16[16,120,128]{2,1,0:T(8,128)(2,1)S(1)} all-to-all(bf16[16,120,128]{2,1,0:T(8,128)(2,1)S(1)} %broadcast_in_dim.30), channel_id=1, replica_groups={{0,8,16,24,32,40,48,56,64,72,80,88,96,104,112,120},{68,76,84,92,100,108..., dimensions={0} | all-to-all | bytes 983040 | tf_op jit(solution)/shard_map/all_to_all | solution.py:310
  163.5 1.7 %collective-permute-start.7 = (bf16[16,120,128]{2,1,0:T(8,128)(2,1)S(1)}, bf16[16,120,128]{2,1,0:T(8,128)(2,1)S(1)}, u32[]{:S(2)}, u32[]{:S(2)}) collective-permute-start(bf16[16,120,128]{2,1,0:T(8,128)(2,1)S(1)} %all_to_all.20), channel_id=1, source_target_pairs={{0,4},{4,0},{8,12},{12,8},{16,20},{20,16},{24,28},{28,24},{32,36},... | collective-permute-start | bytes 1474568 | tf_op jit(solution)/shard_map/ppermute | solution.py:339
  165.2 0.2 reshape.151
  165.4 0.6 convolution_convert_fusion
  166.0 0.6 collective-permute-done.7
  166.7 0.2 reshape.150
  166.9 0.6 broadcast_select_fusion.2
  167.8 0.7 copy.99
  (75 shorter events, 2.4 us)
Async XLA Ops:
  0.6 31.7 %copy-start = (s32[24,16]{0,1:T(8,128)S(1)}, s32[24,16]{0,1:T(8,128)}, u32[]{:S(2)}) copy-start(s32[24,16]{0,1:T(8,128)} %param.22) | copy-start | bytes 4612
  2.3 17.7 %all-to-all-start = ((bf16[16,120,128]{2,1,0:T(8,128)(2,1)}), bf16[16,120,128]{2,1,0:T(8,128)(2,1)S(1)}, u32[]{:S(2)}, u32[]{:S(2)}) async-start(bf16[16,120,128]{2,1,0:T(8,128)(2,1)} %broadcast_in_dim.26), calls=%async_computation | async-start | bytes 983040 | tf_op jit(solution)/shard_map/all_to_all | solution.py:310
  13.3 6.7 %collective-permute-start = (bf16[12,512]{1,0:T(8,128)(2,1)S(1)}, bf16[12,512]{1,0:T(8,128)(2,1)S(1)}, u32[]{:S(2)}, u32[]{:S(2)}) collective-permute-start(bf16[12,512]{1,0:T(8,128)(2,1)S(1)} %constant_dynamic-update-slice_fusion), channel_id=1, source_target_pairs={{0,124},{4,0},{8,4},{12,8},{16,12},{20,16},{24,20},{28,24},{32,28}... | collective-permute-start | bytes 36872 | tf_op jit(solution)/shard_map/ppermute | solution.py:363
  18.7 9.2 %copy-start.10 = (bf16[1280,160]{0,1:T(8,128)(2,1)S(1)}, bf16[1280,160]{0,1:T(8,128)(2,1)}, u32[]{:S(2)}) copy-start(bf16[1280,160]{0,1:T(8,128)(2,1)} %param.17) | copy-start | bytes 1228804
  20.0 107.1 %all-to-all-start.1 = ((bf16[128,256,128]{2,1,0:T(8,128)(2,1)}), bf16[128,256,128]{2,1,0:T(8,128)(2,1)}, u32[]{:S(2)}, u32[]{:S(2)}) async-start(bf16[128,256,128]{2,1,0:T(8,128)(2,1)} %pack.1), calls=%async_computation.1 | async-start | bytes 16777216 | tf_op jit(solution)/shard_map/all_to_all | solution.py:310
  27.9 12.3 %collective-permute-start.4 = (bf16[1280,160]{0,1:T(8,128)(2,1)S(1)}, bf16[1280,160]{0,1:T(8,128)(2,1)S(1)}, u32[]{:S(2)}, u32[]{:S(2)}) collective-permute-start(bf16[1280,160]{0,1:T(8,128)(2,1)S(1)} %copy-done.10), channel_id=1, source_target_pairs={{0,1},{1,2},{2,3},{3,0},{4,5},{5,6},{6,7},{7,4},{8,9},{9,10},{10,1... | collective-permute-start | bytes 1228808 | tf_op jit(solution)/shard_map/ppermute | solution.py:322
  29.2 10.9 %collective-permute-start.6 = (bf16[1280,160]{0,1:T(8,128)(2,1)S(1)}, bf16[1280,160]{0,1:T(8,128)(2,1)S(1)}, u32[]{:S(2)}, u32[]{:S(2)}) collective-permute-start(bf16[1280,160]{0,1:T(8,128)(2,1)S(1)} %copy-done.10), channel_id=1, source_target_pairs={{0,3},{1,0},{2,1},{3,2},{4,7},{5,4},{6,5},{7,6},{8,11},{9,8},{10,9... | collective-permute-start | bytes 1228808 | tf_op jit(solution)/shard_map/ppermute | solution.py:322
  30.7 19.3 %collective-permute-start.5 = (bf16[1280,160]{0,1:T(8,128)(2,1)S(1)}, bf16[1280,160]{0,1:T(8,128)(2,1)S(1)}, u32[]{:S(2)}, u32[]{:S(2)}) collective-permute-start(bf16[1280,160]{0,1:T(8,128)(2,1)S(1)} %copy-done.10), channel_id=1, source_target_pairs={{0,2},{1,3},{2,0},{3,1},{4,6},{5,7},{6,4},{7,5},{8,10},{9,11},{10,... | collective-permute-start | bytes 1228808 | tf_op jit(solution)/shard_map/ppermute | solution.py:322
  50.2 2.6 %collective-permute-start.1 = (bf16[16,120,128]{2,1,0:T(8,128)(2,1)S(1)}, bf16[16,120,128]{2,1,0:T(8,128)(2,1)S(1)}, u32[]{:S(2)}, u32[]{:S(2)}) collective-permute-start(bf16[16,120,128]{2,1,0:T(8,128)(2,1)S(1)} %all-to-all-done), channel_id=1, source_target_pairs={{0,4},{4,0},{8,12},{12,8},{16,20},{20,16},{24,28},{28,24},{32,36},... | collective-permute-start | bytes 1474568 | tf_op jit(solution)/shard_map/ppermute | solution.py:339
  52.8 2.2 %copy-start.2 = (bf16[64,128,2,128]{3,2,1,0:T(2,128)(2,1)S(1)}, bf16[64,128,2,128]{3,2,1,0:T(2,128)(2,1)}, u32[]{:S(2)}) copy-start(bf16[64,128,2,128]{3,2,1,0:T(2,128)(2,1)} %param.15) | copy-start | bytes 12582916
  52.9 2.1 %copy-start.4 = (s32[2048]{0:T(1024)S(1)}, s32[2048]{0:T(1024)}, u32[]{:S(2)}) copy-start(s32[2048]{0:T(1024)} %dst_ref.3) | copy-start | bytes 24580
  53.0 2.1 %copy-start.5 = (s32[2048]{0:T(1024)S(1)}, s32[2048]{0:T(1024)}, u32[]{:S(2)}) copy-start(s32[2048]{0:T(1024)} %req_ref.1) | copy-start | bytes 24580
  53.0 2.1 %copy-start.6 = (s32[2048]{0:T(1024)S(1)}, s32[2048]{0:T(1024)}, u32[]{:S(2)}) copy-start(s32[2048]{0:T(1024)} %idx_ref.1) | copy-start | bytes 24580
  53.0 2.0 %copy-start.7 = (s32[24]{0:T(128)S(1)}, s32[24]{0:T(128)}, u32[]{:S(2)}) copy-start(s32[24]{0:T(128)} %len_ref.1) | copy-start | bytes 292
  55.0 2.2 %copy-start.3 = (bf16[64,128,2,128]{3,2,1,0:T(2,128)(2,1)S(1)}, bf16[64,128,2,128]{3,2,1,0:T(2,128)(2,1)}, u32[]{:S(2)}) copy-start(bf16[64,128,2,128]{3,2,1,0:T(2,128)(2,1)} %param.16) | copy-start | bytes 12582916
  89.0 21.6 %collective-permute-start.2 = (f32[64,2,30]{2,0,1:T(8,128)S(1)}, f32[64,2,30]{2,0,1:T(8,128)S(1)}, u32[]{:S(2)}, u32[]{:S(2)}) collective-permute-start(f32[64,2,30]{2,0,1:T(8,128)S(1)} %get-tuple-element.65), channel_id=1, source_target_pairs={{0,4},{4,0},{8,12},{12,8},{16,20},{20,16},{24,28},{28,24},{32,36},... | collective-permute-start | bytes 46088 | tf_op jit(solution)/shard_map/ppermute | solution.py:339
  106.9 1.9 %copy-start.8 = (f32[4,16,2,30,128]{4,3,2,1,0:T(8,128)S(1)}, f32[4,16,2,30,128]{4,3,2,1,0:T(8,128)}, u32[]{:S(2)}) copy-start(f32[4,16,2,30,128]{4,3,2,1,0:T(8,128)} %reshape.146) | copy-start | bytes 5898244
  109.3 1.0 copy-start.9
  109.8 2.6 %collective-permute-start.3 = (f32[64,30,128]{2,0,1:T(8,128)S(1)}, f32[64,30,128]{2,0,1:T(8,128)S(1)}, u32[]{:S(2)}, u32[]{:S(2)}) collective-permute-start(f32[64,30,128]{2,0,1:T(8,128)S(1)} %copy.88), channel_id=1, source_target_pairs={{0,4},{4,0},{8,12},{12,8},{16,20},{20,16},{24,28},{28,24},{32,36},... | collective-permute-start | bytes 2949128 | tf_op jit(solution)/shard_map/ppermute | solution.py:339
  127.1 21.6 %all-to-all-start.2 = ((bf16[64,32,128]{2,1,0:T(8,128)(2,1)}), bf16[64,32,128]{2,1,0:T(8,128)(2,1)S(1)}, u32[]{:S(2)}, u32[]{:S(2)}) async-start(bf16[64,32,128]{2,1,0:T(8,128)(2,1)} %settle.1), calls=%async_computation.2 | async-start | bytes 1048576 | tf_op jit(solution)/shard_map/all_to_all | solution.py:310
  163.5 3.2 %collective-permute-start.7 = (bf16[16,120,128]{2,1,0:T(8,128)(2,1)S(1)}, bf16[16,120,128]{2,1,0:T(8,128)(2,1)S(1)}, u32[]{:S(2)}, u32[]{:S(2)}) collective-permute-start(bf16[16,120,128]{2,1,0:T(8,128)(2,1)S(1)} %all_to_all.20), channel_id=1, source_target_pairs={{0,4},{4,0},{8,12},{12,8},{16,20},{20,16},{24,28},{28,24},{32,36},... | collective-permute-start | bytes 1474568 | tf_op jit(solution)/shard_map/ppermute | solution.py:339
  166.7 1.8 %copy-start.1 = (s32[24,16]{0,1:T(8,128)S(1)}, s32[24,16]{0,1:T(8,128)}, u32[]{:S(2)}) copy-start(s32[24,16]{0,1:T(8,128)} %param.22) | copy-start | bytes 4612
